TPU v7x, 32 devices: a whole 2x2x4 slice. The times are simulated.
32 devices in a mesh: blk: 8 (over z, x), rep: 4 (over y, core).
Axes of the slice: x: 2, y: 2, z: 4, core: 2. Of those that a mesh axis runs over, the one named last changes fastest.
Arguments:
- samples: bfloat16 [512, 16384], P(None, 'blk'), may hold values from -6 to 6
- theta_tiles: bfloat16 [512, 256, 256], P(('blk', 'rep')), may hold values from -6 to 6
- theta_diag: float32 [16384], P('blk'), may hold values from 0.5 to 2
- tile_row: int32 [512], P(('blk', 'rep')), may hold values from 0 to 63, as said below
- tile_col: int32 [512], P(('blk', 'rep')), may hold values from 0 to 7
- tile_count: int32 [32], P(('blk', 'rep')), may hold values from 4 to 16, as said below
Outputs:
- new_tiles: bfloat16 [512, 256, 256], P(('blk', 'rep'))
- new_diag: float32 [16384], P('blk')
Inputs may be any that keep to these rules, and one draw needn't show every extreme that they name: tile_row[s] differs from the slot's block column j by 1 to 8, of either sign; pairs may repeat, and repeated tiles add. Each device's live slots are its first tile_count slots; in every blk index some device is full.
All inputs are finite; a program needn't handle non-finite values.
Results may differ from a plain program's by a relative error of at most 0.0035.
Values may be sent and summed in bfloat16 or wider, within the bound.
A program may use at most 128 MiB of HBM per device.

v0:
```python
import jax
import jax.numpy as jnp
from jax import lax
from jax.sharding import PartitionSpec as P

B = 256


STEP = 0.25
PENALTY = 0.5


def extended(cells, sides, width):
    for axis, dim in sides:
        count = lax.axis_size(axis)
        ends = count - 1
        head = lax.slice_in_dim(cells, 0, width, axis=dim)
        tail = lax.slice_in_dim(cells, cells.shape[dim] - width, cells.shape[dim], axis=dim)
        cells = jnp.concatenate(
            [
                lax.ppermute(tail, axis, [(i, (i + 1) % count) for i in range(ends)]),
                cells,
                lax.ppermute(head, axis, [((i + 1) % count, i) for i in range(ends)]),
            ],
            axis=dim,
        )
    return cells


def shards(samples, theta_tiles, theta_diag, tile_row, tile_col, tile_count):
    count_ns, width = samples.shape
    blocks = width // B
    slots = theta_tiles.shape[0]
    group = lax.axis_index("blk")
    live = jnp.arange(slots, dtype=jnp.int32) < tile_count[0]
    tiles = jnp.where(live[:, None, None], theta_tiles, jnp.zeros_like(theta_tiles))
    rows = tile_row - (group - 1) * blocks
    onehot = (tile_col[:, None] == jnp.arange(blocks, dtype=jnp.int32)[None, :]).astype(jnp.float32)
    ext_x = extended(samples, (("blk", 1),), width)
    ext_x = ext_x.reshape(count_ns, 3 * blocks, B)
    x_row = jnp.take(ext_x, rows, axis=1)
    prod = jnp.einsum("sta,tab->stb", x_row, tiles, preferred_element_type=jnp.float32)
    partial_image = jnp.einsum(
        "stb,tk->skb", prod, onehot, precision=lax.Precision.HIGHEST
    ).reshape(count_ns, width)
    summed = lax.psum(partial_image, "rep")
    image = (summed + samples.astype(jnp.float32) * theta_diag[None, :]).astype(jnp.bfloat16)
    ext_w = extended(image, (("blk", 1),), width)
    own_image = ext_w[:, width : 2 * width]
    ext_w = ext_w.reshape(count_ns, 3 * blocks, B)
    w_row = jnp.take(ext_w, rows, axis=1)
    x_col = jnp.take(samples.reshape(count_ns, blocks, B), tile_col, axis=1)
    w_col = jnp.take(own_image.reshape(count_ns, blocks, B), tile_col, axis=1)
    first = jnp.einsum("sta,stb->tab", x_row, w_col, preferred_element_type=jnp.float32)
    second = jnp.einsum("sta,stb->tab", w_row, x_col, preferred_element_type=jnp.float32)
    grad = (first + second) / (2.0 * count_ns)
    moved = tiles.astype(jnp.float32) - STEP * grad
    soft_value = jnp.sign(moved) * jnp.maximum(jnp.abs(moved) - STEP * PENALTY, 0.0)
    new_tiles = jnp.where(live[:, None, None], soft_value, jnp.zeros_like(soft_value)).astype(
        jnp.bfloat16
    )
    dots = jnp.sum(samples.astype(jnp.float32) * own_image.astype(jnp.float32), axis=0) / count_ns
    new_diag = theta_diag - STEP * (dots - 1.0 / theta_diag)
    return (new_tiles, new_diag)


def solution(mesh):
    placed = (
        P(None, "blk"),
        P(("blk", "rep"), None, None),
        P("blk"),
        P(("blk", "rep")),
        P(("blk", "rep")),
        P(("blk", "rep")),
    )
    return jax.shard_map(
        shards,
        mesh=mesh,
        in_specs=placed,
        out_specs=(P(("blk", "rep"), None, None), P("blk")),
        check_vma=False,
    )
```

profile of v0, /device:TPU:3, one launch (start us, length us, event | category | flops | bytes accessed | tf_op | source)
XLA Modules:
  0.0 379.2 jit_solution(5847633468776429366)
XLA Ops:
  7.2 0.0 copy-start.5
  7.2 0.0 all-reduce.2.cloned.1.call-start
  7.2 2.9 copy.10
  10.1 3.2 collective-permute-start
  13.3 3.5 collective-permute-start.1
  17.4 0.0 copy-done.5
  17.4 86.1 %collective-permute-done = bf16[512,2048]{0,1:T(8,128)(2,1)} collective-permute-done((bf16[512,2048]{0,1:T(8,128)(2,1)S(1)}, bf16[512,2048]{0,1:T(8,128)(2,1)}, u32[]{:S(2)}, u32[]{:S(2)}) %collective-permute-start) | collective-permute-done | bytes 2097184 | tf_op jit(solution)/shard_map/ppermute | solution.py:21
  103.5 0.0 collective-permute-done.1
  103.5 5.5 %pad_maximum_fusion = bf16[512,6144]{0,1:T(8,128)(2,1)} fusion(bf16[512,2048]{0,1:T(8,128)(2,1)} %collective-permute-done.1, bf16[512,2048]{0,1:T(8,128)(2,1)S(1)} %copy.10, bf16[512,2048]{0,1:T(8,128)(2,1)} %collective-permute-done), kind=kLoop, calls=%fused_computation.4 | loop fusion | flops 18874368 | bytes 12582912 | tf_op jit(solution)/shard_map/concatenate | solution.py:19
  109.0 8.6 %copy.13 = bf16[512,24,256]{2,0,1:T(8,128)(2,1)} copy(bf16[512,24,256]{0,2,1:T(8,128)(2,1)} %bitcast.37) | data formatting | bytes 12582912 | tf_op jit(solution)/shard_map/reshape | solution.py:40
  117.6 5.5 %gather_fusion = bf16[16,512,256]{2,1,0:T(8,128)(2,1)} fusion(bf16[512,24,256]{2,0,1:T(8,128)(2,1)} %copy.13, s32[1024]{0:T(1024)S(1)} %pad_clamp_fusion.1), kind=kCustom, calls=%fused_computation.clone | custom fusion | bytes 8388672 | tf_op jit(solution)/shard_map/jit(_take)/gather | solution.py:41
  123.2 7.6 %fusion.17 = f32[512,16,256]{0,2,1:T(8,128)} fusion(bf16[16,512,256]{2,1,0:T(8,128)(2,1)} %gather_fusion, pred[16]{0:T(512)(128)(4,1)S(1)} %get-tuple-element.6, bf16[16,256,256]{2,1,0:T(8,128)(2,1)} %param.11, pred[16]{0:T(512)(128)(4,1)S(1)} %get-tuple-element.8), kind=kOutput, calls=%fused_computation.27 | convolution fusion | flops 1076887552 | bytes 14680096 | tf_op jit(solution)/shard_map/sta,tab->stb/dot_general | solution.py:42
  130.7 0.0 copy-start.4
  130.7 10.3 %copy.15 = f32[512,16,256]{2,1,0:T(8,128)} copy(f32[512,16,256]{0,2,1:T(8,128)} %fusion.17) | data formatting | bytes 16777216 | tf_op jit(solution)/shard_map/sta,tab->stb/transpose | solution.py:42
  141.0 0.0 copy-done.4
  141.0 8.4 %convolution_bitcast_fusion = f32[512,8,256]{2,1,0:T(8,128)} fusion(f32[512,16,256]{2,1,0:T(8,128)} %copy.15, s32[16]{0:T(128)S(1)} %copy-done.4), kind=kOutput, calls=%fused_computation.28 | convolution fusion | flops 201326720 | bytes 12582976 | tf_op jit(solution)/shard_map/stb,tk->skb/dot_general | solution.py:43
  149.5 5.3 %copy.27 = f32[512,8,256]{0,2,1:T(8,128)} copy(f32[512,8,256]{2,1,0:T(8,128)} %convolution_bitcast_fusion) | data formatting | bytes 8388608 | tf_op jit(solution)/shard_map/reshape | solution.py:45
  154.8 0.0 copy-start.3
  154.8 0.0 all-reduce.2.cloned.1.call-update
  154.8 87.6 %all-reduce.2.cloned.1.call-done = f32[512,2048]{0,1:T(8,128)} async-done(((f32[512,2048]{0,1:T(8,128)}), f32[512,2048]{0,1:T(8,128)}) %all-reduce.2.cloned.1.call-update) | async-done | bytes 4194320 | tf_op jit(solution)/shard_map/psum | solution.py:46
  242.3 0.0 copy-done.3
  242.3 4.7 %fusion.2 = (f32[2048]{0:T(1024)S(1)}, bf16[512,2048]{0,1:T(8,128)(2,1)}) fusion(bf16[512,2048]{0,1:T(8,128)(2,1)S(1)} %copy.10, f32[512,2048]{0,1:T(8,128)} %all-reduce.2.cloned.1.call-done, f32[2048]{0:T(1024)S(1)} %copy-done.3), kind=kLoop, calls=%fused_computation.10 | loop fusion | flops 7337984 | bytes 8404992 | tf_op jit(solution)/shard_map/reduce_sum | solution.py:62
  247.0 3.1 collective-permute-start.2
  250.1 3.7 collective-permute-start.3
  253.8 2.4 copy.22
  256.2 4.4 %gather_fusion.3 = bf16[16,512,256]{2,1,0:T(8,128)(2,1)} fusion(bf16[512,8,256]{2,0,1:T(8,128)(2,1)} %copy.22, s32[1024]{0:T(1024)S(1)} %pad_clamp_fusion), kind=kCustom, calls=%fused_computation.3.clone | custom fusion | bytes 8388672 | tf_op jit(solution)/shard_map/jit(_take)/gather | solution.py:52
  260.6 2.8 copy.18
  263.5 2.7 gather_fusion.1
  266.2 0.6 multiply_subtract_fusion
  266.8 73.7 %collective-permute-done.2 = bf16[512,2048]{0,1:T(8,128)(2,1)} collective-permute-done((bf16[512,2048]{0,1:T(8,128)(2,1)}, bf16[512,2048]{0,1:T(8,128)(2,1)}, u32[]{:S(2)}, u32[]{:S(2)}) %collective-permute-start.2) | collective-permute-done | bytes 2097184 | tf_op jit(solution)/shard_map/ppermute | solution.py:21
  340.5 0.0 collective-permute-done.3
  340.5 5.9 %pad_maximum_fusion.1 = bf16[512,6144]{0,1:T(8,128)(2,1)} fusion(bf16[512,2048]{0,1:T(8,128)(2,1)} %collective-permute-done.3, bf16[512,2048]{0,1:T(8,128)(2,1)} %get-tuple-element.5, bf16[512,2048]{0,1:T(8,128)(2,1)} %collective-permute-done.2), kind=kLoop, calls=%fused_computation.5 | loop fusion | flops 18874368 | bytes 12582912 | tf_op jit(solution)/shard_map/concatenate | solution.py:19
  346.4 8.6 %copy.20 = bf16[512,24,256]{2,0,1:T(8,128)(2,1)} copy(bf16[512,24,256]{0,2,1:T(8,128)(2,1)} %bitcast.36) | data formatting | bytes 12582912 | tf_op jit(solution)/shard_map/reshape | solution.py:50
  355.1 5.5 %gather_fusion.2 = bf16[16,512,256]{2,1,0:T(8,128)(2,1)} fusion(bf16[512,24,256]{2,0,1:T(8,128)(2,1)} %copy.20, s32[1024]{0:T(1024)S(1)} %pad_clamp_fusion.1), kind=kCustom, calls=%fused_computation.2.clone | custom fusion | bytes 8388672 | tf_op jit(solution)/shard_map/jit(_take)/gather | solution.py:51
  360.6 0.0 copy-start
  360.6 0.0 copy-start.1
  360.6 0.0 copy-start.2
  360.6 5.2 %fusion.3 = f32[16,256,256]{2,1,0:T(8,128)S(1)} fusion(bf16[16,512,256]{2,1,0:T(8,128)(2,1)} %gather_fusion.3, bf16[16,512,256]{2,1,0:T(8,128)(2,1)} %gather_fusion.2, pred[16]{0:T(512)(128)(4,1)S(1)} %compare_and_fusion, pred[16]{0:T(512)(128)(4,1)S(1)} %get-tuple-element.6), kind=kOutput, calls=%fused_computation.11 | convolution fusion | flops 1077936128 | bytes 12582944 | tf_op jit(solution)/shard_map/sta,stb->tab/dot_general | solution.py:55
  365.8 0.0 copy-done
  365.8 0.7 copy-done.1
  366.5 0.6 copy-done.2
  367.1 5.2 %select_convert_fusion = bf16[16,256,256]{2,1,0:T(8,128)(2,1)} fusion(f32[16,256,256]{2,1,0:T(8,128)S(1)} %fusion.3, pred[16]{0:T(512)(128)(4,1)S(1)} %get-tuple-element.8, bf16[16,512,256]{2,1,0:T(8,128)(2,1)S(1)} %copy-done.1, pred[16]{0:T(512)(128)(4,1)S(1)} %compare_and_fusion, bf16[16,512,256]{2,1,0:T(8,128)(2,1)S(1)} %copy-done, ...), kind=kOutput, calls=%fused_computation.22 | convolution fusion | flops 1090519040 | bytes 16777264 | tf_op jit(solution)/shard_map/sta,stb->tab/dot_general | solution.py:54
  (5 shorter events, 0.0 us)
Async XLA Ops:
  7.2 10.2 %copy-start.5 = (s32[16]{0:T(128)S(1)}, s32[16]{0:T(128)}, u32[]{:S(2)}) copy-start(s32[16]{0:T(128)} %param.13) | copy-start | bytes 196
  7.2 235.2 %all-reduce.2.cloned.1.call-start = ((), (), s32[]{:S(2)}) async-start(), calls=%async_computation | async-start | bytes 8388608 | tf_op jit(solution)/shard_map/psum | solution.py:46
  10.1 93.4 %collective-permute-start = (bf16[512,2048]{0,1:T(8,128)(2,1)S(1)}, bf16[512,2048]{0,1:T(8,128)(2,1)}, u32[]{:S(2)}, u32[]{:S(2)}) collective-permute-start(bf16[512,2048]{0,1:T(8,128)(2,1)S(1)} %copy.10), channel_id=1, source_target_pairs={{0,4},{4,8},{8,12},{12,16},{16,20},{20,24},{24,28},{1,5},{5,9},{9,... | collective-permute-start | bytes 6291464 | tf_op jit(solution)/shard_map/ppermute | solution.py:21
  13.3 90.3 %collective-permute-start.1 = (bf16[512,2048]{0,1:T(8,128)(2,1)S(1)}, bf16[512,2048]{0,1:T(8,128)(2,1)}, u32[]{:S(2)}, u32[]{:S(2)}) collective-permute-start(bf16[512,2048]{0,1:T(8,128)(2,1)S(1)} %copy.10), channel_id=1, source_target_pairs={{4,0},{8,4},{12,8},{16,12},{20,16},{24,20},{28,24},{5,1},{9,5},{13... | collective-permute-start | bytes 6291464 | tf_op jit(solution)/shard_map/ppermute | solution.py:23
  130.7 10.3 %copy-start.4 = (s32[16]{0:T(128)S(1)}, s32[16]{0:T(128)}, u32[]{:S(2)}) copy-start(s32[16]{0:T(128)} %param.14) | copy-start | bytes 196
  154.8 87.6 %copy-start.3 = (f32[2048]{0:T(1024)S(1)}, f32[2048]{0:T(1024)}, u32[]{:S(2)}) copy-start(f32[2048]{0:T(1024)} %param.12) | copy-start | bytes 24580
  247.0 93.5 %collective-permute-start.2 = (bf16[512,2048]{0,1:T(8,128)(2,1)}, bf16[512,2048]{0,1:T(8,128)(2,1)}, u32[]{:S(2)}, u32[]{:S(2)}) collective-permute-start(bf16[512,2048]{0,1:T(8,128)(2,1)} %get-tuple-element.5), channel_id=1, source_target_pairs={{0,4},{4,8},{8,12},{12,16},{16,20},{20,24},{24,28},{1,5},{5,9},{9,... | collective-permute-start | bytes 6291464 | tf_op jit(solution)/shard_map/ppermute | solution.py:21
  250.1 90.4 %collective-permute-start.3 = (bf16[512,2048]{0,1:T(8,128)(2,1)}, bf16[512,2048]{0,1:T(8,128)(2,1)}, u32[]{:S(2)}, u32[]{:S(2)}) collective-permute-start(bf16[512,2048]{0,1:T(8,128)(2,1)} %get-tuple-element.5), channel_id=1, source_target_pairs={{4,0},{8,4},{12,8},{16,12},{20,16},{24,20},{28,24},{5,1},{9,5},{13... | collective-permute-start | bytes 6291464 | tf_op jit(solution)/shard_map/ppermute | solution.py:23
  360.6 5.2 %copy-start = (bf16[16,512,256]{2,1,0:T(8,128)(2,1)S(1)}, bf16[16,512,256]{2,1,0:T(8,128)(2,1)}, u32[]{:S(2)}) copy-start(bf16[16,512,256]{2,1,0:T(8,128)(2,1)} %gather_fusion) | copy-start | bytes 12582916
  360.6 5.9 %copy-start.1 = (bf16[16,512,256]{2,1,0:T(8,128)(2,1)S(1)}, bf16[16,512,256]{2,1,0:T(8,128)(2,1)}, u32[]{:S(2)}) copy-start(bf16[16,512,256]{2,1,0:T(8,128)(2,1)} %gather_fusion.1) | copy-start | bytes 12582916
  360.6 6.5 %copy-start.2 = (bf16[16,256,256]{2,1,0:T(8,128)(2,1)S(1)}, bf16[16,256,256]{2,1,0:T(8,128)(2,1)}, u32[]{:S(2)}) copy-start(bf16[16,256,256]{2,1,0:T(8,128)(2,1)} %param.11) | copy-start | bytes 6291460
Sparse Core Ops, SparseCore 0:
  154.9 87.4 all-reduce.1
where the time goes:
time: 383 us; the launch traced here: 379 us
  waiting for transfers between devices  247 us (64%)
  local copies, waits for them, and re-layouts  60.5 us (16%)
  matrix products  26.4 us (7%)
  other arithmetic  16.7 us (4%)
  between operations  14.8 us (4%)
  starting transfers between devices  13.4 us (3%)
    ppermute x2, waiting for transfers between devices, extended(): lax.ppermute(tail, axis, [(i, (i + 1) % count) for i in range(ends)])  160 us
    psum x1, waiting for transfers between devices, shards(): summed = lax.psum(partial_image, 'rep')  87.6 us
    concatenate x2, other arithmetic, extended(): jnp.concatenate([lax.ppermute(tail, axis, [(i, (i + 1) % count) for i in...  11.4 us
    transpose x1, local copies, waits for them, and re-layouts, shards(): jnp.einsum('sta,tab->stb', x_row, tiles, preferred_element_type=jnp.float32)  10.3 us
    reshape x1, local copies, waits for them, and re-layouts, shards(): ext_x = ext_x.reshape(count_ns, 3 * blocks, B)  8.63 us
    reshape x1, local copies, waits for them, and re-layouts, shards(): ext_w = ext_w.reshape(count_ns, 3 * blocks, B)  8.63 us
    dot_general x1, matrix products, shards(): jnp.einsum('stb,tk->skb', prod, onehot, precision=lax.Precision.HIGHEST)  8.41 us
  transfers between devices with their start and end apart: 5, of which 3 were waited for; matrix products, arithmetic and copies ran while one was open for 3% of the time, Pallas kernels for 0%

commit v1 on v0

v1 whole, which is shorter than its diff:
```python
import functools

import jax
import jax.numpy as jnp
from jax import lax
from jax.experimental import pallas as pl
from jax.experimental.pallas import tpu as pltpu
from jax.sharding import PartitionSpec as P

B = 256
STEP = 0.25
PENALTY = 0.5
VMEM_BYTES = 48 * 1024 * 1024
STRIP = 16


class Place:
    def __init__(self, groups):
        self.g = lax.axis_index("blk")
        self.r = lax.axis_index("rep")
        self.parity = self.g % 2
        self.core = self.r % 2
        self.half = self.r // 2
        self.partner = self.g + 1 - 2 * self.parity
        self.target = self.g + 2 - 4 * self.parity
        self.source = self.g - 2 + 4 * self.parity
        self.has_target = jnp.logical_and(self.target >= 0, self.target < groups)
        self.has_source = jnp.logical_and(self.source >= 0, self.source < groups)
        self.near = 2 * (1 - self.parity)
        self.far = 2 * self.parity

    def to_partner(self):
        return {"blk": self.partner, "rep": self.r}

    def to_target(self):
        return {"blk": self.target, "rep": self.r}

    def to_source(self):
        return {"blk": self.source, "rep": self.r}

    def to_core(self):
        return {"blk": self.g, "rep": self.r + 1 - 2 * self.core}

    def to_half(self):
        return {"blk": self.g, "rep": self.r + 2 - 4 * self.half}

    def greet(self):
        barrier = pltpu.get_barrier_semaphore()

        def signal(device):
            pl.semaphore_signal(
                barrier, inc=1, device_id=device, device_id_type=pl.DeviceIdType.MESH
            )

        signal(self.to_partner())
        signal(self.to_core())
        signal(self.to_half())

        @pl.when(self.has_target)
        def _():
            signal(self.to_target())

        @pl.when(self.has_source)
        def _():
            signal(self.to_source())

        peers = 3 + jnp.where(self.has_target, 1, 0) + jnp.where(self.has_source, 1, 0)
        pl.semaphore_wait(barrier, peers)


def remote(src, dst, send, recv, at, device):
    return pltpu.make_async_remote_copy(
        src_ref=src,
        dst_ref=dst,
        send_sem=send.at[at],
        recv_sem=recv.at[at],
        device_id=device,
        device_id_type=pl.DeviceIdType.MESH,
    )


def halo_kernel(groups, x, ext, own_sem, send, recv):
    here = Place(groups)
    unit = x.shape[0] // 8
    shared = 6 * here.half + here.core
    theirs = 6 * (1 - here.half) + here.core
    chunks = [shared, 2 + 2 * here.core, 3 + 2 * here.core]

    def rows(chunk):
        return pl.ds(pl.multiple_of(chunk * unit, unit), unit)

    def ext_at(section, chunk):
        return ext.at[section, rows(chunk), :]

    own = pltpu.make_async_copy(x, ext.at[1], own_sem)
    own.start()
    here.greet()
    near, far = here.near, here.far
    partner = [
        remote(x.at[rows(c), :], ext_at(far, c), send, recv, k, here.to_partner())
        for k, c in enumerate(chunks)
    ]
    relay = [
        remote(ext_at(near, c), ext_at(far, c), send, recv, 3 + k, here.to_target())
        for k, c in enumerate(chunks)
    ]
    across = [
        remote(ext_at(s, shared), ext_at(s, shared), send, recv, 6 + k, here.to_half())
        for k, s in enumerate([near, far])
    ]
    share_near = [
        remote(ext_at(near, c), ext_at(near, c), send, recv, 8 + k, here.to_core())
        for k, c in enumerate(chunks + [theirs])
    ]
    share_far = [
        remote(ext_at(far, c), ext_at(far, c), send, recv, 12 + k, here.to_core())
        for k, c in enumerate(chunks + [theirs])
    ]
    for copy in partner:
        copy.start()
    for k in range(3):
        partner[k].wait_recv()

        @pl.when(here.has_target)
        def _():
            relay[k].start()

        if k == 0:
            across[0].start()
        share_near[k].start()

    @pl.when(here.has_source)
    def _():
        for k in range(3):
            relay[k].wait_recv()
            if k == 0:
                across[1].start()
            share_far[k].start()

    across[0].wait_recv()
    share_near[3].start()

    @pl.when(here.has_source)
    def _():
        across[1].wait_recv()
        share_far[3].start()
        for copy in share_far:
            copy.wait_recv()
        for copy in share_far:
            copy.wait_send()
        across[1].wait_send()

    for copy in share_near:
        copy.wait_recv()
    for copy in partner + share_near + [across[0]]:
        copy.wait_send()

    @pl.when(here.has_target)
    def _():
        for copy in relay:
            copy.wait_send()

    own.wait()


def halo(x, groups):
    count, width = x.shape
    return pl.pallas_call(
        functools.partial(halo_kernel, groups),
        out_shape=jax.ShapeDtypeStruct((3, count, width), x.dtype),
        in_specs=[pl.BlockSpec(memory_space=pl.ANY)],
        out_specs=pl.BlockSpec(memory_space=pl.ANY),
        scratch_shapes=[
            pltpu.SemaphoreType.DMA,
            pltpu.SemaphoreType.DMA((16,)),
            pltpu.SemaphoreType.DMA((16,)),
        ],
        compiler_params=pltpu.CompilerParams(collective_id=0, has_side_effects=True),
        name="halo",
    )(x)


def image_kernel(slots, row, col, count, x_row, tile, out, total):
    s = pl.program_id(0)
    blocks = total.shape[0]

    @pl.when(s == 0)
    def _():
        total[...] = jnp.zeros_like(total)

    @pl.when(s < count[0])
    def _():
        total[col[s]] += jnp.dot(x_row[0], tile[0], preferred_element_type=jnp.float32)

    @pl.when(s == slots - 1)
    def _():
        for k in range(blocks):
            out[:, k * B : (k + 1) * B] = total[k].astype(out.dtype)


def partial_image(ext, tiles, row, col, count):
    _, samples, width = ext.shape
    slots = tiles.shape[0]
    blocks = width // B
    return pl.pallas_call(
        functools.partial(image_kernel, slots),
        grid_spec=pltpu.PrefetchScalarGridSpec(
            num_scalar_prefetch=3,
            grid=(slots,),
            in_specs=[
                pl.BlockSpec((1, samples, B), lambda s, row, col, n: (row[s] // blocks, 0, row[s] % blocks)),
                pl.BlockSpec((1, B, B), lambda s, row, col, n: (s, 0, 0)),
            ],
            out_specs=pl.BlockSpec((samples, width), lambda s, row, col, n: (0, 0)),
            scratch_shapes=[pltpu.VMEM((blocks, samples, B), jnp.float32)],
        ),
        out_shape=jax.ShapeDtypeStruct((samples, width), jnp.bfloat16),
        compiler_params=pltpu.CompilerParams(vmem_limit_bytes=VMEM_BYTES),
        name="partial_image",
    )(row, col, count, ext, tiles)


def reduce_kernel(groups, part, x, diag, ext, x_mine, core_in, chip_sum, half_in, final, x_sem, own_sem, send, recv):
    here = Place(groups)
    count = part.shape[0]
    quarter = count // 4
    unit = quarter // 2
    mine = 2 * here.half + here.core
    other = 2 * (1 - here.half) + here.core
    mine_core = 2 * here.half + 1 - here.core
    other_core = 2 * (1 - here.half) + 1 - here.core

    def start_row(q, k):
        return pl.multiple_of(q * quarter + k * unit, unit)

    def rows(q, k):
        return pl.ds(start_row(q, k), unit)

    def ext_at(section, q, k):
        return ext.at[section, rows(q, k), :]

    load = pltpu.make_async_copy(
        x.at[pl.ds(pl.multiple_of(mine * quarter, quarter), quarter), :], x_mine, x_sem
    )
    load.start()
    here.greet()
    near, far = here.near, here.far
    to_core = [
        remote(part.at[rows(q, k), :], core_in.at[j, k], send, recv, 2 * j + k, here.to_core())
        for j, q in enumerate([other_core, mine_core])
        for k in range(2)
    ]
    to_half = [
        remote(chip_sum.at[k], half_in.at[k], send, recv, 4 + k, here.to_half()) for k in range(2)
    ]
    gather = [
        remote(final.at[k], ext_at(1, mine, k), send, recv, 6 + k, here.to_half()) for k in range(2)
    ]
    partner = [
        remote(final.at[k], ext_at(far, mine, k), send, recv, 8 + k, here.to_partner()) for k in range(2)
    ] + [
        remote(ext_at(1, other, k), ext_at(far, other, k), send, recv, 10 + k, here.to_partner())
        for k in range(2)
    ]
    places = [(mine, 0), (mine, 1), (other, 0), (other, 1)]
    relay = [
        remote(ext_at(near, q, k), ext_at(far, q, k), send, recv, 12 + i, here.to_target())
        for i, (q, k) in enumerate(places)
    ]
    share_own = [
        remote(
            final.at[k] if i < 2 else ext_at(1, q, k), ext_at(1, q, k), send, recv, 16 + i, here.to_core()
        )
        for i, (q, k) in enumerate(places)
    ]
    share_near = [
        remote(ext_at(near, q, k), ext_at(near, q, k), send, recv, 20 + i, here.to_core())
        for i, (q, k) in enumerate(places)
    ]
    share_far = [
        remote(ext_at(far, q, k), ext_at(far, q, k), send, recv, 24 + i, here.to_core())
        for i, (q, k) in enumerate(places)
    ]
    own = [pltpu.make_async_copy(final.at[k], ext_at(1, mine, k), own_sem.at[k]) for k in range(2)]

    for copy in to_core:
        copy.start()
    for k in range(2):
        to_core[k].wait_recv()

        @pl.loop(0, unit // STRIP)
        def _(i):
            at = pl.ds(pl.multiple_of(i * STRIP, STRIP), STRIP)
            from_part = pl.ds(pl.multiple_of(start_row(other, k) + i * STRIP, STRIP), STRIP)
            both = part[from_part, :].astype(jnp.float32) + core_in[0, k, at, :].astype(jnp.float32)
            chip_sum[k, at, :] = both.astype(jnp.bfloat16)

        to_half[k].start()
    load.wait()
    for k in range(2):
        to_core[2 + k].wait_recv()
        to_half[k].wait_recv()

        @pl.loop(0, unit // STRIP)
        def _(i):
            at = pl.ds(pl.multiple_of(i * STRIP, STRIP), STRIP)
            from_part = pl.ds(pl.multiple_of(start_row(mine, k) + i * STRIP, STRIP), STRIP)
            from_x = pl.ds(pl.multiple_of(k * unit + i * STRIP, STRIP), STRIP)
            both = part[from_part, :].astype(jnp.float32) + core_in[1, k, at, :].astype(jnp.float32)
            both = both + half_in[k, at, :].astype(jnp.float32)
            final[k, at, :] = (both + x_mine[from_x, :].astype(jnp.float32) * diag[...]).astype(jnp.bfloat16)

        gather[k].start()
        partner[k].start()
        share_own[k].start()
        own[k].start()
    for k in range(2):
        gather[k].wait_recv()
        partner[2 + k].start()
        share_own[2 + k].start()
        partner[k].wait_recv()

        @pl.when(here.has_target)
        def _():
            relay[k].start()

        share_near[k].start()
    for k in range(2, 4):
        partner[k].wait_recv()

        @pl.when(here.has_target)
        def _():
            relay[k].start()

        share_near[k].start()

    @pl.when(here.has_source)
    def _():
        for k in range(4):
            relay[k].wait_recv()
            share_far[k].start()
        for copy in share_far:
            copy.wait_recv()
        for copy in share_far:
            copy.wait_send()

    for copy in share_own + share_near:
        copy.wait_recv()
    for copy in to_core + to_half + gather + partner + share_own + share_near:
        copy.wait_send()

    @pl.when(here.has_target)
    def _():
        for copy in relay:
            copy.wait_send()

    for copy in own:
        copy.wait()


def whole_image(part, x, diag, groups):
    count, width = x.shape
    quarter = count // 4
    unit = quarter // 2
    return pl.pallas_call(
        functools.partial(reduce_kernel, groups),
        out_shape=jax.ShapeDtypeStruct((3, count, width), jnp.bfloat16),
        in_specs=[
            pl.BlockSpec(memory_space=pltpu.VMEM),
            pl.BlockSpec(memory_space=pl.ANY),
            pl.BlockSpec(memory_space=pltpu.VMEM),
        ],
        out_specs=pl.BlockSpec(memory_space=pl.ANY),
        scratch_shapes=[
            pltpu.VMEM((quarter, width), jnp.bfloat16),
            pltpu.VMEM((2, 2, unit, width), jnp.bfloat16),
            pltpu.VMEM((2, unit, width), jnp.bfloat16),
            pltpu.VMEM((2, unit, width), jnp.bfloat16),
            pltpu.VMEM((2, unit, width), jnp.bfloat16),
            pltpu.SemaphoreType.DMA,
            pltpu.SemaphoreType.DMA((2,)),
            pltpu.SemaphoreType.DMA((28,)),
            pltpu.SemaphoreType.DMA((28,)),
        ],
        compiler_params=pltpu.CompilerParams(
            collective_id=1, has_side_effects=True, vmem_limit_bytes=VMEM_BYTES
        ),
        name="whole_image",
    )(part, x, diag)


def grad_kernel(scale, row, col, count, x_row, w_row, x_col, w_col, tile, out):
    s = pl.program_id(0)
    live = s < count[0]

    @pl.when(live)
    def _():
        dims = (((0,), (0,)), ((), ()))
        grad = lax.dot_general(x_row[0], w_col[0], dims, preferred_element_type=jnp.float32)
        grad += lax.dot_general(w_row[0], x_col[0], dims, preferred_element_type=jnp.float32)
        moved = tile[0].astype(jnp.float32) - (STEP * scale) * grad
        kept = jnp.maximum(jnp.abs(moved) - STEP * PENALTY, 0.0)
        out[0] = jnp.where(moved < 0, -kept, kept).astype(out.dtype)

    @pl.when(jnp.logical_not(live))
    def _():
        out[...] = jnp.zeros_like(out)


def update(ext_x, ext_w, tiles, row, col, count):
    _, samples, width = ext_x.shape
    slots = tiles.shape[0]
    blocks = width // B
    by_row = pl.BlockSpec((1, samples, B), lambda s, row, col, n: (row[s] // blocks, 0, row[s] % blocks))
    by_col = pl.BlockSpec((1, samples, B), lambda s, row, col, n: (1, 0, col[s]))
    by_slot = pl.BlockSpec((1, B, B), lambda s, row, col, n: (s, 0, 0))
    return pl.pallas_call(
        functools.partial(grad_kernel, 1.0 / (2.0 * samples)),
        grid_spec=pltpu.PrefetchScalarGridSpec(
            num_scalar_prefetch=3,
            grid=(slots,),
            in_specs=[by_row, by_row, by_col, by_col, by_slot],
            out_specs=by_slot,
        ),
        out_shape=jax.ShapeDtypeStruct(tiles.shape, jnp.bfloat16),
        compiler_params=pltpu.CompilerParams(vmem_limit_bytes=VMEM_BYTES),
        name="update",
    )(row, col, count, ext_x, ext_w, ext_x, ext_w, tiles)


def shards(samples, theta_tiles, theta_diag, tile_row, tile_col, tile_count):
    count_ns, width = samples.shape
    blocks = width // B
    groups = lax.axis_size("blk")
    group = lax.axis_index("blk")
    rows = jnp.clip(tile_row - (group - 1) * blocks, 0, 3 * blocks - 1)
    ext_x = halo(samples, groups)
    part = partial_image(ext_x, theta_tiles, rows, tile_col, tile_count)
    ext_w = whole_image(part, samples, theta_diag[None, :], groups)
    new_tiles = update(ext_x, ext_w, theta_tiles, rows, tile_col, tile_count)
    dots = jnp.sum(samples.astype(jnp.float32) * ext_w[1].astype(jnp.float32), axis=0) / count_ns
    new_diag = theta_diag - STEP * (dots - 1.0 / theta_diag)
    return (new_tiles, new_diag)


def solution(mesh):
    placed = (
        P(None, "blk"),
        P(("blk", "rep"), None, None),
        P("blk"),
        P(("blk", "rep")),
        P(("blk", "rep")),
        P(("blk", "rep")),
    )
    return jax.shard_map(
        shards,
        mesh=mesh,
        in_specs=placed,
        out_specs=(P(("blk", "rep"), None, None), P("blk")),
        check_vma=False,
    )
```

time: 383 us -> 147 us (0.38)
  waiting for transfers between devices: 247 us -> 0 us
  Pallas kernels: 0 us -> 141 us
  local copies, waits for them, and re-layouts: 60.5 us -> 0.02 us
  matrix products: 26.4 us -> 0 us
  between operations: 14.8 us -> 1.35 us
  starting transfers between devices: 13.4 us -> 0 us
  other arithmetic: 16.7 us -> 3.55 us
    ppermute x4 -> x0, waiting for transfers between devices: 160 us -> none  [the longest x2 160 us: extended(): lax.ppermute(tail, axis, [(i, (i + 1) % count) for i in range(ends)])]
    pallas_call x0 -> x4, Pallas kernels: none -> 141 us  [the longest x1 64.9 us: halo(): pl.pallas_call(functools.partial(halo_kernel, groups), out_shape=jax.Shap...]
    psum x1 -> x0, waiting for transfers between devices: 87.6 us -> none  [shards(): summed = lax.psum(partial_image, 'rep')]
    reshape x5 -> x0, local copies, waits for them, and re-layouts: 27.8 us -> none  [the longest x1 8.63 us: shards(): ext_x = ext_x.reshape(count_ns, 3 * blocks, B)]
    dot_general x4 -> x0, matrix products: 26.4 us -> none  [the longest x1 8.41 us: shards(): jnp.einsum('stb,tk->skb', prod, onehot, precision=lax.Precision.HIGHEST)]
    gather x4 -> x0, local copies, waits for them, and re-layouts: 18.2 us -> none  [the longest x1 5.54 us: shards(): w_row = jnp.take(ext_w, rows, axis=1)]
    ppermute x4 -> x0, starting transfers between devices: 13.4 us -> none  [the longest x2 7.13 us: extended(): lax.ppermute(head, axis, [((i + 1) % count, i) for i in range(ends)])]
    concatenate x2 -> x0, other arithmetic: 11.4 us -> none  [extended(): jnp.concatenate([lax.ppermute(tail, axis, [(i, (i + 1) % count) for i in...]
  transfers between devices with their start and end apart: 5 -> 0, of which waited for: 3 -> 0; matrix products, arithmetic and copies ran while one was open for 3% -> 0% of each run, Pallas kernels for 0% -> 0%
where the time goes in v1:
time: 147 us; the launch traced here: 146 us
  Pallas kernels  141 us (96%)
  other arithmetic  3.55 us (2%)
    pallas_call x1, Pallas kernels, halo(): pl.pallas_call(functools.partial(halo_kernel, groups), out_shape=jax.Shap...  64.9 us
    pallas_call x1, Pallas kernels, whole_image(): pl.pallas_call(functools.partial(reduce_kernel, groups), out_shape=jax.Sh...  49.9 us
    pallas_call x1, Pallas kernels, update(): pl.pallas_call(functools.partial(grad_kernel, 1.0 / (2.0 * samples)), gri...  15.2 us
    pallas_call x1, Pallas kernels, partial_image(): pl.pallas_call(functools.partial(image_kernel, slots), grid_spec=pltpu.Pr...  11.3 us

profile of v1, /device:TPU:3, one launch (start us, length us, event | category | flops | bytes accessed | tf_op | source)
XLA Modules:
  0.0 146.3 jit_solution(6450840317127499395)
XLA Ops:
  1.3 0.7 subtract_clamp_fusion.row
  1.9 0.0 copy-start.1
  1.9 0.0 copy-start.3
  1.9 64.9 %halo.1.x_row.x_col = bf16[3,512,2048]{2,1,0:T(8,128)(2,1)} custom-call(bf16[512,2048]{1,0:T(8,128)(2,1)} %x.3), custom_call_target="tpu_custom_call" | custom-call | tf_op jit(solution)/shard_map/halo/pallas_call | solution.py:168
  66.9 0.0 copy-done.1
  66.9 0.0 copy-done.3
  66.9 0.0 copy-start
  66.9 0.0 copy-start.2
  66.9 11.3 %partial_image.1.part = bf16[512,2048]{1,0:T(8,128)(2,1)S(1)} custom-call(s32[16]{0:T(128)S(1)} %subtract_clamp_fusion.row, s32[16]{0:T(128)S(1)} %copy-done.3, s32[1]{0:T(128)S(6)} %copy.8.count, bf16[3,512,2048]{2,1,0:T(8,128)(2,1)} %halo.1.x_row.x_col, bf16[16,256,256]{2,1,0:T(8,128)(2,1)S(1)} %copy-done.1), custom_call_target="tpu_custom_call" | custom-call | tf_op jit(solution)/shard_map/partial_image/pallas_call | solution.py:205
  78.2 0.0 copy-done
  78.2 0.0 copy-done.2
  78.2 49.9 %whole_image.1.w_row.w_col = bf16[3,512,2048]{2,1,0:T(8,128)(2,1)} custom-call(bf16[512,2048]{1,0:T(8,128)(2,1)S(1)} %partial_image.1.part, bf16[512,2048]{1,0:T(8,128)(2,1)S(1)} %copy-done, f32[1,2048]{1,0:T(1,128)S(1)} %bitcast.4), custom_call_target="tpu_custom_call" | custom-call | tf_op jit(solution)/shard_map/whole_image/pallas_call | solution.py:365
  128.2 15.2 %update.1 = bf16[16,256,256]{2,1,0:T(8,128)(2,1)} custom-call(s32[16]{0:T(128)S(1)} %subtract_clamp_fusion.row, s32[16]{0:T(128)S(1)} %copy-done.3, s32[1]{0:T(128)S(6)} %copy.8.count, bf16[3,512,2048]{2,1,0:T(8,128)(2,1)} %halo.1.x_row.x_col, bf16[3,512,2048]{2,1,0:T(8,128)(2,1)} %whole_image.1.w_row.w_col, bf16[3,512,2048]{2,1,0:T(8,128)(2,1)} %halo.1.x_row.x_col, ...), custom_call_target="tpu_custom_call" | custom-call | tf_op jit(solution)/shard_map/update/pallas_call | solution.py:417
  143.4 2.3 %fusion = f32[2048]{0:T(1024)S(1)} fusion(bf16[512,2048]{1,0:T(8,128)(2,1)S(1)} %copy-done, bf16[3,512,2048]{2,1,0:T(8,128)(2,1)} %whole_image.1.w_row.w_col), kind=kLoop, calls=%fused_computation.1 | loop fusion | flops 4192256 | bytes 4202496 | tf_op jit(solution)/shard_map/reduce_sum | solution.py:441
  145.7 0.6 multiply_subtract_fusion
Async XLA Ops:
  1.9 64.9 %copy-start.1 = (bf16[16,256,256]{2,1,0:T(8,128)(2,1)S(1)}, bf16[16,256,256]{2,1,0:T(8,128)(2,1)}, u32[]{:S(2)}) copy-start(bf16[16,256,256]{2,1,0:T(8,128)(2,1)} %tile.3) | copy-start | bytes 6291460
  1.9 64.9 %copy-start.3 = (s32[16]{0:T(128)S(1)}, s32[16]{0:T(128)}, u32[]{:S(2)}) copy-start(s32[16]{0:T(128)} %col.3) | copy-start | bytes 196
  66.9 11.3 %copy-start = (bf16[512,2048]{1,0:T(8,128)(2,1)S(1)}, bf16[512,2048]{1,0:T(8,128)(2,1)}, u32[]{:S(2)}) copy-start(bf16[512,2048]{1,0:T(8,128)(2,1)} %x.3) | copy-start | bytes 6291460
  66.9 11.3 %copy-start.2 = (f32[2048]{0:T(1024)S(1)}, f32[2048]{0:T(1024)}, u32[]{:S(2)}) copy-start(f32[2048]{0:T(1024)} %param.8) | copy-start | bytes 24580

commit v2 on v0

v2 whole, which is shorter than its diff:
```python
import functools

import jax
import jax.numpy as jnp
from jax import lax
from jax.experimental import pallas as pl
from jax.experimental.pallas import tpu as pltpu
from jax.sharding import PartitionSpec as P

B = 256
STEP = 0.25
PENALTY = 0.5
VMEM_BYTES = 52 * 1024 * 1024


class Place:
    def __init__(self, groups):
        self.g = lax.axis_index("blk")
        self.r = lax.axis_index("rep")
        self.parity = self.g % 2
        self.core = self.r % 2
        self.half = self.r // 2
        self.partner = self.g + 1 - 2 * self.parity
        self.target = self.g + 2 - 4 * self.parity
        self.source = self.g - 2 + 4 * self.parity
        self.has_target = jnp.logical_and(self.target >= 0, self.target < groups)
        self.has_source = jnp.logical_and(self.source >= 0, self.source < groups)
        self.near = 2 * (1 - self.parity)
        self.far = 2 * self.parity

    def to_partner(self):
        return {"blk": self.partner, "rep": self.r}

    def to_target(self):
        return {"blk": self.target, "rep": self.r}

    def to_source(self):
        return {"blk": self.source, "rep": self.r}

    def to_core(self):
        return {"blk": self.g, "rep": self.r + 1 - 2 * self.core}

    def to_half(self):
        return {"blk": self.g, "rep": self.r + 2 - 4 * self.half}

    def greet(self):
        barrier = pltpu.get_barrier_semaphore()

        def signal(device):
            pl.semaphore_signal(
                barrier, inc=1, device_id=device, device_id_type=pl.DeviceIdType.MESH
            )

        signal(self.to_partner())
        signal(self.to_core())
        signal(self.to_half())

        @pl.when(self.has_target)
        def _():
            signal(self.to_target())

        @pl.when(self.has_source)
        def _():
            signal(self.to_source())

        peers = 3 + jnp.where(self.has_target, 1, 0) + jnp.where(self.has_source, 1, 0)
        pl.semaphore_wait(barrier, peers)


def remote(src, dst, send, recv, at, device):
    return pltpu.make_async_remote_copy(
        src_ref=src,
        dst_ref=dst,
        send_sem=send.at[at],
        recv_sem=recv.at[at],
        device_id=device,
        device_id_type=pl.DeviceIdType.MESH,
    )


def step_kernel(
    groups, row, prev, last, col, live, x, tiles_in, diag, out, diag_out,
    ext, img, own_img, tiles, acc, part, core_in, chip_sum, half_in, x_turned, moved, dots, dots_in,
    x_sem, tile_sem, send, recv,
):
    here = Place(groups)
    slots = tiles.shape[0]
    samples = x.shape[0]
    blocks = x.shape[1] // B
    pair = blocks // 2
    unit = samples // 8
    scale = STEP / (2.0 * samples)
    near, far = here.near, here.far

    loads = [
        pltpu.make_async_copy(x.at[:, k * B : (k + 1) * B], ext.at[blocks + k], x_sem.at[k])
        for k in range(blocks)
    ]
    for load in loads:
        load.start()
    tile_load = pltpu.make_async_copy(tiles_in, tiles, tile_sem)
    tile_load.start()
    acc[0] = jnp.zeros_like(acc[0])
    here.greet()

    shared = 6 * here.half + here.core
    theirs = 6 * (1 - here.half) + here.core
    chunks = [shared, 2 + 2 * here.core, 3 + 2 * here.core]

    def x_at(section, chunk):
        return ext.at[pl.ds(section * blocks, blocks), pl.ds(pl.multiple_of(chunk * unit, unit), unit), :]

    partner = [
        remote(x_at(1, c), x_at(far, c), send, recv, k, here.to_partner()) for k, c in enumerate(chunks)
    ]
    relay = [
        remote(x_at(near, c), x_at(far, c), send, recv, 3 + k, here.to_target())
        for k, c in enumerate(chunks)
    ]
    across = [
        remote(x_at(s, shared), x_at(s, shared), send, recv, 6 + k, here.to_half())
        for k, s in enumerate([near, far])
    ]
    share_near = [
        remote(x_at(near, c), x_at(near, c), send, recv, 8 + k, here.to_core())
        for k, c in enumerate(chunks + [theirs])
    ]
    share_far = [
        remote(x_at(far, c), x_at(far, c), send, recv, 12 + k, here.to_core())
        for k, c in enumerate(chunks + [theirs])
    ]
    for load in loads:
        load.wait()
    for copy in partner:
        copy.start()
    for k in range(3):
        partner[k].wait_recv()

        @pl.when(here.has_target)
        def _():
            relay[k].start()

        if k == 0:
            across[0].start()
        share_near[k].start()

    @pl.when(here.has_source)
    def _():
        for k in range(3):
            relay[k].wait_recv()
            if k == 0:
                across[1].start()
            share_far[k].start()

    across[0].wait_recv()
    share_near[3].start()

    @pl.when(here.has_source)
    def _():
        across[1].wait_recv()
        share_far[3].start()
        for copy in share_far:
            copy.wait_recv()
        for copy in share_far:
            copy.wait_send()
        across[1].wait_send()

    for copy in share_near:
        copy.wait_recv()
    for copy in partner + share_near + [across[0]]:
        copy.wait_send()

    @pl.when(here.has_target)
    def _():
        for copy in relay:
            copy.wait_send()

    tile_load.wait()

    @pl.loop(0, slots)
    def _(s):
        acc[s + 1] = acc[prev[s]] + jnp.dot(ext[row[s]], tiles[s], preferred_element_type=jnp.float32)

    quarter = samples // 4
    mine = 2 * here.half + here.core
    other = 2 * (1 - here.half) + here.core
    mine_core = 2 * here.half + 1 - here.core
    other_core = 2 * (1 - here.half) + 1 - here.core

    def rows(q):
        return pl.ds(pl.multiple_of(q * quarter, quarter), quarter)

    def part_at(q, h):
        return part.at[pl.ds(h * pair, pair), rows(q), :]

    def img_at(section, q, h):
        return img.at[pl.ds(section * blocks + h * pair, pair), q]

    def own_at(q, h):
        return own_img.at[pl.ds(h * pair, pair), q]

    to_core = [
        remote(part_at(q, h), core_in.at[j, h], send, recv, 16 + 2 * j + h, here.to_core())
        for j, q in enumerate([other_core, mine_core])
        for h in range(2)
    ]
    to_half = [
        remote(chip_sum.at[h], half_in.at[h], send, recv, 20 + h, here.to_half()) for h in range(2)
    ]
    gather = [
        remote(own_at(mine, h), own_at(mine, h), send, recv, 22 + h, here.to_half())
        for h in range(2)
    ]
    places = [(mine, 0), (mine, 1), (other, 0), (other, 1)]
    partner_w = [
        remote(own_at(q, h), img_at(far, q, h), send, recv, 24 + i, here.to_partner())
        for i, (q, h) in enumerate(places)
    ]
    relay_w = [
        remote(img_at(near, q, h), img_at(far, q, h), send, recv, 28 + i, here.to_target())
        for i, (q, h) in enumerate(places)
    ]
    share_own_w = [
        remote(own_at(q, h), own_at(q, h), send, recv, 32 + i, here.to_core())
        for i, (q, h) in enumerate(places)
    ]
    share_near_w, share_far_w = [
        [
            remote(img_at(s, q, h), img_at(s, q, h), send, recv, first + i, here.to_core())
            for i, (q, h) in enumerate(places)
        ]
        for s, first in [(near, 36), (far, 40)]
    ]
    dots_core = remote(dots.at[0], dots_in.at[0], send, recv, 44, here.to_core())
    dots_half = remote(dots.at[1], dots_in.at[1], send, recv, 45, here.to_half())

    for h in range(2):

        @pl.loop(h * pair, (h + 1) * pair)
        def _(k):
            part[k] = acc[last[k]].astype(jnp.bfloat16)

        to_core[h].start()
        to_core[2 + h].start()
    for h in range(2):
        to_core[h].wait_recv()

        @pl.loop(0, pair)
        def _(j):
            both = part[h * pair + j, rows(other), :].astype(jnp.float32) + core_in[0, h, j].astype(jnp.float32)
            chip_sum[h, j] = both.astype(jnp.bfloat16)

        to_half[h].start()

    @pl.loop(0, slots)
    def _(s):
        x_turned[s] = ext[row[s]].T

    for h in range(2):
        to_core[2 + h].wait_recv()
        to_half[h].wait_recv()
        for j in range(pair):
            k = h * pair + j
            lanes = pl.ds(k * B, B)
            xs = ext[blocks + k, rows(mine), :].astype(jnp.float32)
            both = part[k, rows(mine), :].astype(jnp.float32) + core_in[1, h, j].astype(jnp.float32)
            both = both + half_in[h, j].astype(jnp.float32) + xs * diag[:, lanes]
            rounded = both.astype(jnp.bfloat16)
            own_img[k, mine] = rounded.T
            dots[0, k : k + 1, :] = jnp.sum(xs * rounded.astype(jnp.float32), axis=0, keepdims=True)
        gather[h].start()
        partner_w[h].start()
        share_own_w[h].start()
    dots_core.start()
    for h in range(2):
        gather[h].wait_recv()
        partner_w[2 + h].start()
        share_own_w[2 + h].start()
        partner_w[h].wait_recv()

        @pl.when(here.has_target)
        def _():
            relay_w[h].start()

        share_near_w[h].start()
    dots_core.wait_recv()
    dots[1] = dots[0] + dots_in[0]
    dots_half.start()
    for copy in share_own_w:
        copy.wait_recv()

    def turned(ref, at):
        return jnp.concatenate([ref[at, q] for q in range(4)], axis=1)

    def first_half(start, end):
        @pl.loop(start, end)
        def _(s):
            grad = lax.dot_general(
                x_turned[s], turned(own_img, col[s]), (((1,), (1,)), ((), ())),
                preferred_element_type=jnp.float32,
            )
            moved[s] = tiles[s].astype(jnp.float32) - scale * grad

    first_half(0, slots // 2)

    @pl.loop(0, blocks)
    def _(k):
        img[blocks + k] = own_img[k]

    partner_w[2].wait_recv()

    @pl.when(here.has_target)
    def _():
        relay_w[2].start()

    share_near_w[2].start()
    first_half(slots // 2, slots)
    partner_w[3].wait_recv()

    @pl.when(here.has_target)
    def _():
        relay_w[3].start()

    share_near_w[3].start()
    dots_half.wait_recv()
    for k in range(blocks):
        lanes = pl.ds(k * B, B)
        total = dots[1, k : k + 1, :] + dots_in[1, k : k + 1, :]
        old = diag[:, lanes]
        diag_out[:, lanes] = old - STEP * (total / samples - 1.0 / old)

    @pl.when(here.has_source)
    def _():
        for i in range(4):
            relay_w[i].wait_recv()
            share_far_w[i].start()
        for copy in share_far_w:
            copy.wait_recv()

    for copy in share_near_w:
        copy.wait_recv()

    @pl.loop(0, slots)
    def _(s):
        grad = jnp.dot(turned(img, row[s]), ext[blocks + col[s]], preferred_element_type=jnp.float32)
        value = moved[s] - scale * grad
        kept = jnp.maximum(jnp.abs(value) - STEP * PENALTY, 0.0)
        signed = jnp.where(value < 0, -kept, kept)
        out[s] = jnp.where(s < live[0], signed, 0.0).astype(out.dtype)

    for copy in to_core + to_half + gather + partner_w + share_own_w + share_near_w + [dots_core, dots_half]:
        copy.wait_send()

    @pl.when(here.has_target)
    def _():
        for copy in relay_w:
            copy.wait_send()

    @pl.when(here.has_source)
    def _():
        for copy in share_far_w:
            copy.wait_send()


def step(x, tiles, diag, row, prev, last, col, live, groups):
    samples, width = x.shape
    slots = tiles.shape[0]
    blocks = width // B
    pair = blocks // 2
    quarter = samples // 4
    bf16, f32 = jnp.bfloat16, jnp.float32
    smem = pl.BlockSpec(memory_space=pltpu.SMEM)
    vmem = pl.BlockSpec(memory_space=pltpu.VMEM)
    hbm = pl.BlockSpec(memory_space=pl.ANY)
    return pl.pallas_call(
        functools.partial(step_kernel, groups),
        out_shape=(
            jax.ShapeDtypeStruct(tiles.shape, bf16),
            jax.ShapeDtypeStruct(diag.shape, f32),
        ),
        in_specs=[smem, smem, smem, smem, smem, hbm, hbm, vmem],
        out_specs=(vmem, vmem),
        scratch_shapes=[
            pltpu.VMEM((3 * blocks, samples, B), bf16),
            pltpu.VMEM((3 * blocks, 4, B, quarter), bf16),
            pltpu.VMEM((blocks, 4, B, quarter), bf16),
            pltpu.VMEM(tiles.shape, bf16),
            pltpu.VMEM((slots + 1, samples, B), f32),
            pltpu.VMEM((blocks, samples, B), bf16),
            pltpu.VMEM((2, 2, pair, quarter, B), bf16),
            pltpu.VMEM((2, pair, quarter, B), bf16),
            pltpu.VMEM((2, pair, quarter, B), bf16),
            pltpu.VMEM((slots, B, samples), bf16),
            pltpu.VMEM((slots, B, B), f32),
            pltpu.VMEM((2, blocks, B), f32),
            pltpu.VMEM((2, blocks, B), f32),
            pltpu.SemaphoreType.DMA((blocks,)),
            pltpu.SemaphoreType.DMA,
            pltpu.SemaphoreType.DMA((46,)),
            pltpu.SemaphoreType.DMA((46,)),
        ],
        compiler_params=pltpu.CompilerParams(
            collective_id=0, has_side_effects=True, vmem_limit_bytes=VMEM_BYTES
        ),
        name="step",
    )(row, prev, last, col, live, x, tiles, diag)


def shards(samples, theta_tiles, theta_diag, tile_row, tile_col, tile_count):
    blocks = samples.shape[1] // B
    slots = theta_tiles.shape[0]
    groups = lax.axis_size("blk")
    group = lax.axis_index("blk")
    rows = jnp.clip(tile_row - (group - 1) * blocks, 0, 3 * blocks - 1)
    at = jnp.arange(slots, dtype=jnp.int32)
    linked = jnp.where(at < tile_count[0], at + 1, 0)
    same = jnp.logical_and(tile_col[:, None] == tile_col[None, :], at[None, :] < at[:, None])
    prev = jnp.max(jnp.where(same, linked[None, :], 0), axis=1)
    hit = tile_col[None, :] == jnp.arange(blocks, dtype=jnp.int32)[:, None]
    last = jnp.max(jnp.where(hit, linked[None, :], 0), axis=1)
    new_tiles, new_diag = step(
        samples, theta_tiles, theta_diag[None, :], rows, prev, last, tile_col, tile_count, groups
    )
    return (new_tiles, new_diag[0])


def solution(mesh):
    placed = (
        P(None, "blk"),
        P(("blk", "rep"), None, None),
        P("blk"),
        P(("blk", "rep")),
        P(("blk", "rep")),
        P(("blk", "rep")),
    )
    return jax.shard_map(
        shards,
        mesh=mesh,
        in_specs=placed,
        out_specs=(P(("blk", "rep"), None, None), P("blk")),
        check_vma=False,
    )
```

time: 383 us -> 95.6 us (0.25)
  waiting for transfers between devices: 247 us -> 0 us
  Pallas kernels: 0 us -> 86.6 us
  local copies, waits for them, and re-layouts: 60.5 us -> 5.04 us
  matrix products: 26.4 us -> 0 us
  other arithmetic: 16.7 us -> 2.35 us
  between operations: 14.8 us -> 1.3 us
  starting transfers between devices: 13.4 us -> 0 us
    ppermute x4 -> x0, waiting for transfers between devices: 160 us -> none  [the longest x2 160 us: extended(): lax.ppermute(tail, axis, [(i, (i + 1) % count) for i in range(ends)])]
    psum x1 -> x0, waiting for transfers between devices: 87.6 us -> none  [shards(): summed = lax.psum(partial_image, 'rep')]
    pallas_call x0 -> x1, Pallas kernels: none -> 86.6 us  [step(): pl.pallas_call(functools.partial(step_kernel, groups), out_shape=(jax.Sha...]
    reshape x5 -> x0, local copies, waits for them, and re-layouts: 27.8 us -> none  [the longest x1 8.63 us: shards(): ext_x = ext_x.reshape(count_ns, 3 * blocks, B)]
    dot_general x4 -> x0, matrix products: 26.4 us -> none  [the longest x1 8.41 us: shards(): jnp.einsum('stb,tk->skb', prod, onehot, precision=lax.Precision.HIGHEST)]
    gather x4 -> x0, local copies, waits for them, and re-layouts: 18.2 us -> none  [the longest x1 5.54 us: shards(): w_row = jnp.take(ext_w, rows, axis=1)]
    ppermute x4 -> x0, starting transfers between devices: 13.4 us -> none  [the longest x2 7.13 us: extended(): lax.ppermute(head, axis, [((i + 1) % count, i) for i in range(ends)])]
    concatenate x2 -> x0, other arithmetic: 11.4 us -> none  [extended(): jnp.concatenate([lax.ppermute(tail, axis, [(i, (i + 1) % count) for i in...]
  transfers between devices with their start and end apart: 5 -> 0, of which waited for: 3 -> 0; matrix products, arithmetic and copies ran while one was open for 3% -> 0% of each run, Pallas kernels for 0% -> 0%
where the time goes in v2:
time: 95.6 us; the launch traced here: 95.2 us
  Pallas kernels  86.6 us (91%)
  local copies, waits for them, and re-layouts  5.04 us (5%)
  other arithmetic  2.35 us (2%)
  between operations  1.3 us (1%)
    pallas_call x1, Pallas kernels, step(): pl.pallas_call(functools.partial(step_kernel, groups), out_shape=(jax.Sha...  86.6 us
    unnamed x6, local copies, waits for them, and re-layouts  5.04 us

profile of v2, /device:TPU:3, one launch (start us, length us, event | category | flops | bytes accessed | tf_op | source)
XLA Modules:
  0.0 95.2 jit_solution(12261047847960079722)
XLA Ops:
  1.3 0.7 subtract_clamp_fusion.row
  1.9 0.8 select_reduce_fusion.1.last
  2.7 0.9 select_reduce_fusion.prev
  3.6 0.0 copy-start
  3.6 0.7 copy-done
  4.3 0.0 copy-start.1
  4.3 0.7 copy-done.1
  5.0 86.6 %step.1 = (bf16[16,256,256]{2,1,0:T(8,128)(2,1)}, f32[1,2048]{1,0:T(1,128)S(1)}) custom-call(s32[16]{0:T(128)S(1)} %subtract_clamp_fusion.row, s32[16]{0:T(128)S(1)} %select_reduce_fusion.prev, s32[8]{0:T(128)S(1)} %select_reduce_fusion.1.last, s32[16]{0:T(128)S(1)} %copy-done.1, s32[1]{0:T(128)} %copy.10.live, bf16[512,2048]{1,0:T(8,128)(2,1)} %x.1, ...), custom_call_target="tpu_custom_call" | custom-call | tf_op jit(solution)/shard_map/step/pallas_call | solution.py:375
  91.6 3.1 %copy.11 = bf16[16,256,256]{2,1,0:T(8,128)(2,1)} copy(bf16[16,256,256]{2,1,0:T(8,128)(2,1)} %get-tuple-element.8) | data formatting | bytes 4194304
  94.6 0.6 copy.12
  (1 shorter events, 0.0 us)
Async XLA Ops:
  3.6 0.7 copy-start
  4.3 0.7 copy-start.1

commit v3 on v0

v3 whole, which is shorter than its diff:
```python
import functools

import jax
import jax.numpy as jnp
from jax import lax
from jax.experimental import pallas as pl
from jax.experimental.pallas import tpu as pltpu
from jax.sharding import PartitionSpec as P

B = 256
STEP = 0.25
PENALTY = 0.5
VMEM_BYTES = 40 * 1024 * 1024


class Place:
    def __init__(self, groups):
        self.g = lax.axis_index("blk")
        self.r = lax.axis_index("rep")
        self.parity = self.g % 2
        self.core = self.r % 2
        self.half = self.r // 2
        self.partner = self.g + 1 - 2 * self.parity
        self.target = self.g + 2 - 4 * self.parity
        self.source = self.g - 2 + 4 * self.parity
        self.has_target = jnp.logical_and(self.target >= 0, self.target < groups)
        self.has_source = jnp.logical_and(self.source >= 0, self.source < groups)
        self.near = 2 * (1 - self.parity)
        self.far = 2 * self.parity

    def to_partner(self):
        return {"blk": self.partner, "rep": self.r}

    def to_target(self):
        return {"blk": self.target, "rep": self.r}

    def to_source(self):
        return {"blk": self.source, "rep": self.r}

    def to_core(self):
        return {"blk": self.g, "rep": self.r + 1 - 2 * self.core}

    def to_half(self):
        return {"blk": self.g, "rep": self.r + 2 - 4 * self.half}

    def greet(self):
        barrier = pltpu.get_barrier_semaphore()

        def signal(device):
            pl.semaphore_signal(
                barrier, inc=1, device_id=device, device_id_type=pl.DeviceIdType.MESH
            )

        signal(self.to_partner())
        signal(self.to_core())
        signal(self.to_half())

        @pl.when(self.has_target)
        def _():
            signal(self.to_target())

        @pl.when(self.has_source)
        def _():
            signal(self.to_source())

        peers = 3 + jnp.where(self.has_target, 1, 0) + jnp.where(self.has_source, 1, 0)
        pl.semaphore_wait(barrier, peers)


def remote(src, dst, send, recv, at, device):
    return pltpu.make_async_remote_copy(
        src_ref=src,
        dst_ref=dst,
        send_sem=send.at[at],
        recv_sem=recv.at[at],
        device_id=device,
        device_id_type=pl.DeviceIdType.MESH,
    )


HALVES = 2
COPIES = 42


class Half:
    def __init__(self, here, first, ext, img, own_img, part, core_in, chip_sum, half_in, send, recv):
        self.here = here
        self.ext, self.img, self.own_img = ext, img, own_img
        self.part, self.core_in, self.chip_sum, self.half_in = part, core_in, chip_sum, half_in
        blocks, samples, _ = part.shape
        unit = samples // 8
        near, far = here.near, here.far
        self.mine = 2 * here.half + here.core
        self.other = 2 * (1 - here.half) + here.core
        self.mine_core = 2 * here.half + 1 - here.core
        self.other_core = 2 * (1 - here.half) + 1 - here.core
        self.owned = blocks // 4
        owned = self.owned

        def copy(src, dst, at, device):
            return remote(src, dst, send, recv, first + at, device)

        shared = 6 * here.half + here.core
        theirs = 6 * (1 - here.half) + here.core
        chunks = [shared, 2 + 2 * here.core, 3 + 2 * here.core]

        def x_at(section, chunk):
            rows = pl.ds(pl.multiple_of(chunk * unit, unit), unit)
            return ext.at[pl.ds(section * blocks, blocks), rows, :]

        self.partner = [
            copy(x_at(1, c), x_at(far, c), k, here.to_partner()) for k, c in enumerate(chunks)
        ]
        self.relay = [
            copy(x_at(near, c), x_at(far, c), 3 + k, here.to_target()) for k, c in enumerate(chunks)
        ]
        self.across = [
            copy(x_at(s, shared), x_at(s, shared), 6 + k, here.to_half()) for k, s in enumerate([near, far])
        ]
        self.share_near, self.share_far = [
            [copy(x_at(s, c), x_at(s, c), at + k, here.to_core()) for k, c in enumerate(chunks + [theirs])]
            for s, at in [(near, 8), (far, 12)]
        ]

        def img_at(section, q, e):
            return img.at[section * blocks + q * owned + e]

        def own_at(q, e):
            return own_img.at[q * owned + e]

        self.to_core = [
            copy(part.at[pl.ds(q * owned, owned)], core_in.at[j], 16 + j, here.to_core())
            for j, q in enumerate([self.other_core, self.mine_core])
        ]
        self.to_half = [copy(chip_sum.at[e], half_in.at[e], 18 + e, here.to_half()) for e in range(2)]
        self.gather = [
            copy(own_at(self.mine, e), own_at(self.mine, e), 20 + e, here.to_half()) for e in range(2)
        ]
        places = [(self.mine, 0), (self.mine, 1), (self.other, 0), (self.other, 1)]
        self.partner_w = [
            copy(own_at(q, e), img_at(far, q, e), 22 + i, here.to_partner())
            for i, (q, e) in enumerate(places)
        ]
        self.relay_w = [
            copy(img_at(near, q, e), img_at(far, q, e), 26 + i, here.to_target())
            for i, (q, e) in enumerate(places)
        ]
        self.share_own_w = [
            copy(own_at(q, e), own_at(q, e), 30 + i, here.to_core()) for i, (q, e) in enumerate(places)
        ]
        self.share_near_w, self.share_far_w = [
            [
                copy(img_at(s, q, e), img_at(s, q, e), at + i, here.to_core())
                for i, (q, e) in enumerate(places)
            ]
            for s, at in [(near, 34), (far, 38)]
        ]

    def send_x(self):
        for copy in self.partner:
            copy.start()

    def pass_x(self, k):
        self.partner[k].wait_recv()

        @pl.when(self.here.has_target)
        def _():
            self.relay[k].start()

        if k == 0:
            self.across[0].start()
        self.share_near[k].start()

    def end_x(self):
        @pl.when(self.here.has_source)
        def _():
            for k in range(3):
                self.relay[k].wait_recv()
                if k == 0:
                    self.across[1].start()
                self.share_far[k].start()

        self.across[0].wait_recv()
        self.share_near[3].start()

        @pl.when(self.here.has_source)
        def _():
            self.across[1].wait_recv()
            self.share_far[3].start()
            for copy in self.share_far:
                copy.wait_recv()

        for copy in self.share_near:
            copy.wait_recv()

    def sum_slots(self, acc, row, prev, last, tiles):
        @pl.loop(0, tiles.shape[0])
        def _(s):
            product = jnp.dot(self.ext[row[s]], tiles[s], preferred_element_type=jnp.float32)
            acc[s + 1] = acc[prev[s]] + product

        for j, q in enumerate([self.other_core, self.mine_core, self.other, self.mine]):
            for e in range(2):
                k = q * self.owned + e
                self.part[k] = acc[last[k]].astype(jnp.bfloat16)
            if j < 2:
                self.to_core[j].start()

    def sum_chip(self):
        self.to_core[0].wait_recv()
        for e in range(2):
            both = self.part[self.other * self.owned + e].astype(jnp.float32)
            both = both + self.core_in[0, e].astype(jnp.float32)
            self.chip_sum[e] = both.astype(jnp.bfloat16)
            self.to_half[e].start()

    def finish_image(self, diag, dots):
        self.to_core[1].wait_recv()
        blocks = self.part.shape[0]
        for e in range(2):
            self.to_half[e].wait_recv()
            k = self.mine * self.owned + e
            xs = self.ext[blocks + k].astype(jnp.float32)
            both = self.part[k].astype(jnp.float32) + self.core_in[1, e].astype(jnp.float32)
            both = both + self.half_in[e].astype(jnp.float32) + xs * diag[pl.ds(k, 1), :]
            rounded = both.astype(jnp.bfloat16)
            self.own_img[k] = rounded.T
            self.partner_w[e].start()
            self.gather[e].start()
            self.share_own_w[e].start()
            dots[0, pl.ds(k, 1), :] += jnp.sum(xs * rounded.astype(jnp.float32), axis=0, keepdims=True)

    def pass_gathered(self, e):
        self.gather[e].wait_recv()
        self.partner_w[2 + e].start()
        self.share_own_w[2 + e].start()

    def pass_w(self, i):
        self.partner_w[i].wait_recv()

        @pl.when(self.here.has_target)
        def _():
            self.relay_w[i].start()

        self.share_near_w[i].start()

    def end_own_w(self):
        for copy in self.share_own_w:
            copy.wait_recv()
        blocks = self.part.shape[0]

        @pl.loop(0, blocks)
        def _(k):
            self.img[blocks + k] = self.own_img[k]

    def end_w(self):
        @pl.when(self.here.has_source)
        def _():
            for i in range(4):
                self.relay_w[i].wait_recv()
                self.share_far_w[i].start()
            for copy in self.share_far_w:
                copy.wait_recv()

        for copy in self.share_near_w:
            copy.wait_recv()

    def drain(self):
        for copies in [
            self.partner, self.share_near, self.across[:1], self.to_core, self.to_half, self.gather,
            self.partner_w, self.share_own_w, self.share_near_w,
        ]:
            for copy in copies:
                copy.wait_send()

        @pl.when(self.here.has_target)
        def _():
            for copy in self.relay + self.relay_w:
                copy.wait_send()

        @pl.when(self.here.has_source)
        def _():
            for copy in self.share_far + self.across[1:] + self.share_far_w:
                copy.wait_send()


def step_kernel(
    groups, row_in, col, live, x, tiles_in, diag_in, out, diag_out,
    ext_a, ext_b, img_a, img_b, own_a, own_b, part_a, part_b, core_a, core_b, chip_a, chip_b, half_a, half_b,
    tiles, acc, x_turned, moved, diag_flat, diag, dots, dots_in, row, prev, last,
    x_sem, tile_sem, diag_sem, send, recv,
):
    here = Place(groups)
    slots = tiles.shape[0]
    samples = x.shape[0]
    blocks = x.shape[1] // B
    cut = samples // HALVES
    scale = STEP / (2.0 * samples)
    a = Half(here, 0, ext_a, img_a, own_a, part_a, core_a, chip_a, half_a, send, recv)
    b = Half(here, COPIES, ext_b, img_b, own_b, part_b, core_b, chip_b, half_b, send, recv)
    dots_core = remote(dots.at[0], dots_in.at[0], send, recv, 2 * COPIES, here.to_core())
    dots_half = remote(dots.at[1], dots_in.at[1], send, recv, 2 * COPIES + 1, here.to_half())

    loads = [
        [
            pltpu.make_async_copy(
                x.at[h * cut : (h + 1) * cut, k * B : (k + 1) * B], half.ext.at[blocks + k], x_sem.at[h, k]
            )
            for k in range(blocks)
        ]
        for h, half in enumerate([a, b])
    ]
    for load in loads[0] + loads[1]:
        load.start()
    diag_load = pltpu.make_async_copy(diag_in, diag_flat, diag_sem)
    diag_load.start()
    tile_load = pltpu.make_async_copy(tiles_in, tiles, tile_sem)
    tile_load.start()
    here.greet()
    for load in loads[0]:
        load.wait()
    a.send_x()

    def latest(column, end):
        def later(t, best):
            return jnp.where(jnp.logical_and(t < live[0], col[t] == column), t + 1, best)

        return lax.fori_loop(0, end, later, jnp.int32(0))

    @pl.loop(0, slots)
    def _(s):
        row[s] = jnp.clip(row_in[s] - (here.g - 1) * blocks, 0, 3 * blocks - 1)
        prev[s] = latest(col[s], s)

    @pl.loop(0, blocks)
    def _(k):
        last[k] = latest(k, slots)

    acc[0] = jnp.zeros_like(acc[0])
    dots[0] = jnp.zeros_like(dots[0])
    diag_load.wait()
    for k in range(blocks):
        diag[k : k + 1, :] = diag_flat[:, k * B : (k + 1) * B]
    for load in loads[1]:
        load.wait()
    tile_load.wait()

    def turn(half, at):
        @pl.loop(0, slots)
        def _(s):
            x_turned[at, s] = half.ext[row[s]].T

    def own_grad(half, at, s):
        return lax.dot_general(
            x_turned[at, s], half.own_img[col[s]], (((1,), (1,)), ((), ())),
            preferred_element_type=jnp.float32,
        )

    def row_grad(half, s):
        return jnp.dot(half.img[row[s]], half.ext[blocks + col[s]], preferred_element_type=jnp.float32)

    for k in range(3):
        a.pass_x(k)
    b.send_x()
    a.end_x()
    b.pass_x(0)
    a.sum_slots(acc, row, prev, last, tiles)
    b.pass_x(1)
    a.sum_chip()
    b.pass_x(2)
    turn(a, 0)
    b.end_x()
    b.sum_slots(acc, row, prev, last, tiles)
    a.finish_image(diag, dots)
    b.sum_chip()
    for e in range(2):
        a.pass_gathered(e)
        a.pass_w(e)
    turn(b, 1)
    b.finish_image(diag, dots)
    dots_core.start()
    a.pass_w(2)
    a.pass_w(3)
    for e in range(2):
        b.pass_gathered(e)
        b.pass_w(e)
    dots_core.wait_recv()
    dots[1] = dots[0] + dots_in[0]
    dots_half.start()
    a.end_own_w()
    a.end_w()

    def first_half(start, end):
        @pl.loop(start, end)
        def _(s):
            moved[s] = tiles[s].astype(jnp.float32) - scale * (own_grad(a, 0, s) + row_grad(a, s))

    first_half(0, slots // 2)
    b.pass_w(2)
    first_half(slots // 2, slots)
    b.pass_w(3)
    b.end_own_w()

    @pl.loop(0, slots)
    def _(s):
        moved[s] -= scale * own_grad(b, 1, s)

    dots_half.wait_recv()
    for k in range(blocks):
        total = dots[1, k : k + 1, :] + dots_in[1, k : k + 1, :]
        old = diag[k : k + 1, :]
        diag_out[:, k * B : (k + 1) * B] = old - STEP * (total / samples - 1.0 / old)
    b.end_w()

    @pl.loop(0, slots)
    def _(s):
        value = moved[s] - scale * row_grad(b, s)
        kept = jnp.maximum(jnp.abs(value) - STEP * PENALTY, 0.0)
        signed = jnp.where(value < 0, -kept, kept)
        out[s] = jnp.where(s < live[0], signed, 0.0).astype(out.dtype)

    a.drain()
    b.drain()
    dots_core.wait_send()
    dots_half.wait_send()


def step(x, tiles, diag, row, col, live, groups):
    samples, width = x.shape
    slots = tiles.shape[0]
    blocks = width // B
    owned = blocks // 4
    cut = samples // HALVES
    bf16, f32 = jnp.bfloat16, jnp.float32
    smem = pl.BlockSpec(memory_space=pltpu.SMEM)
    vmem = pl.BlockSpec(memory_space=pltpu.VMEM)
    hbm = pl.BlockSpec(memory_space=pl.ANY)

    def twice(*shape):
        return [pltpu.VMEM(shape, bf16)] * 2

    return pl.pallas_call(
        functools.partial(step_kernel, groups),
        out_shape=(
            jax.ShapeDtypeStruct(tiles.shape, bf16),
            jax.ShapeDtypeStruct(diag.shape, f32),
        ),
        in_specs=[smem, smem, smem, hbm, hbm, hbm],
        out_specs=(vmem, vmem),
        scratch_shapes=twice(3 * blocks, cut, B)
        + twice(3 * blocks, B, cut)
        + twice(blocks, B, cut)
        + twice(blocks, cut, B)
        + twice(2, owned, cut, B)
        + twice(owned, cut, B)
        + twice(owned, cut, B)
        + [
            pltpu.VMEM(tiles.shape, bf16),
            pltpu.VMEM((slots + 1, cut, B), f32),
            pltpu.VMEM((2, slots, B, cut), bf16),
            pltpu.VMEM((slots, B, B), f32),
            pltpu.VMEM(diag.shape, f32),
            pltpu.VMEM((blocks, B), f32),
            pltpu.VMEM((2, blocks, B), f32),
            pltpu.VMEM((2, blocks, B), f32),
            pltpu.SMEM((slots,), jnp.int32),
            pltpu.SMEM((slots,), jnp.int32),
            pltpu.SMEM((blocks,), jnp.int32),
            pltpu.SemaphoreType.DMA((2, blocks)),
            pltpu.SemaphoreType.DMA,
            pltpu.SemaphoreType.DMA,
            pltpu.SemaphoreType.DMA((2 * COPIES + 2,)),
            pltpu.SemaphoreType.DMA((2 * COPIES + 2,)),
        ],
        compiler_params=pltpu.CompilerParams(
            collective_id=0, has_side_effects=True, vmem_limit_bytes=VMEM_BYTES
        ),
        name="step",
    )(row, col, live, x, tiles, diag)


def shards(samples, theta_tiles, theta_diag, tile_row, tile_col, tile_count):
    groups = lax.axis_size("blk")
    new_tiles, new_diag = step(
        samples, theta_tiles, theta_diag[None, :], tile_row, tile_col, tile_count, groups
    )
    return (new_tiles, new_diag[0])


def solution(mesh):
    placed = (
        P(None, "blk"),
        P(("blk", "rep"), None, None),
        P("blk"),
        P(("blk", "rep")),
        P(("blk", "rep")),
        P(("blk", "rep")),
    )
    return jax.shard_map(
        shards,
        mesh=mesh,
        in_specs=placed,
        out_specs=(P(("blk", "rep"), None, None), P("blk")),
        check_vma=False,
    )
```

time: 383 us -> 85.4 us (0.22)
  waiting for transfers between devices: 247 us -> 0 us
  Pallas kernels: 0 us -> 76.8 us
  local copies, waits for them, and re-layouts: 60.5 us -> 7.1 us
  matrix products: 26.4 us -> 0 us
  other arithmetic: 16.7 us -> 0 us
  between operations: 14.8 us -> 1.3 us
  starting transfers between devices: 13.4 us -> 0 us
    ppermute x4 -> x0, waiting for transfers between devices: 160 us -> none  [the longest x2 160 us: extended(): lax.ppermute(tail, axis, [(i, (i + 1) % count) for i in range(ends)])]
    psum x1 -> x0, waiting for transfers between devices: 87.6 us -> none  [shards(): summed = lax.psum(partial_image, 'rep')]
    pallas_call x0 -> x1, Pallas kernels: none -> 76.8 us  [step(): pl.pallas_call(functools.partial(step_kernel, groups), out_shape=(jax.Sha...]
    reshape x5 -> x0, local copies, waits for them, and re-layouts: 27.8 us -> none  [the longest x1 8.63 us: shards(): ext_x = ext_x.reshape(count_ns, 3 * blocks, B)]
    dot_general x4 -> x0, matrix products: 26.4 us -> none  [the longest x1 8.41 us: shards(): jnp.einsum('stb,tk->skb', prod, onehot, precision=lax.Precision.HIGHEST)]
    gather x4 -> x0, local copies, waits for them, and re-layouts: 18.2 us -> none  [the longest x1 5.54 us: shards(): w_row = jnp.take(ext_w, rows, axis=1)]
    ppermute x4 -> x0, starting transfers between devices: 13.4 us -> none  [the longest x2 7.13 us: extended(): lax.ppermute(head, axis, [((i + 1) % count, i) for i in range(ends)])]
    concatenate x2 -> x0, other arithmetic: 11.4 us -> none  [extended(): jnp.concatenate([lax.ppermute(tail, axis, [(i, (i + 1) % count) for i in...]
  transfers between devices with their start and end apart: 5 -> 0, of which waited for: 3 -> 0; matrix products, arithmetic and copies ran while one was open for 3% -> 0% of each run, Pallas kernels for 0% -> 0%
where the time goes in v3:
time: 85.4 us; the launch traced here: 85.2 us
  Pallas kernels  76.8 us (90%)
  local copies, waits for them, and re-layouts  7.1 us (8%)
  between operations  1.3 us (2%)
    pallas_call x1, Pallas kernels, step(): pl.pallas_call(functools.partial(step_kernel, groups), out_shape=(jax.Sha...  76.8 us
    unnamed x12, local copies, waits for them, and re-layouts  7.1 us

profile of v3, /device:TPU:3, one launch (start us, length us, event | category | flops | bytes accessed | tf_op | source)
XLA Modules:
  0.0 85.2 jit_solution(7821067650714849251)
XLA Ops:
  1.3 0.0 copy-start
  1.3 1.6 %copy-done = bf16[512,2048]{1,0:T(8,128)(2,1)S(1)} copy-done((bf16[512,2048]{1,0:T(8,128)(2,1)S(1)}, bf16[512,2048]{1,0:T(8,128)(2,1)}, u32[]{:S(2)}) %copy-start) | copy-done | bytes 2097176
  2.9 0.0 copy-start.1
  2.9 1.6 %copy-done.1 = bf16[16,256,256]{2,1,0:T(8,128)(2,1)S(1)} copy-done((bf16[16,256,256]{2,1,0:T(8,128)(2,1)S(1)}, bf16[16,256,256]{2,1,0:T(8,128)(2,1)}, u32[]{:S(2)}) %copy-start.1) | copy-done | bytes 2097176
  4.5 0.0 copy-start.2
  4.5 0.7 copy-done.2
  5.2 0.0 copy-start.3
  5.2 0.7 copy-done.3
  5.8 0.0 copy-start.4
  5.8 0.7 copy-done.4
  6.5 76.8 %step.1 = (bf16[16,256,256]{2,1,0:T(8,128)(2,1)S(1)}, f32[1,2048]{1,0:T(1,128)S(1)}) custom-call(s32[16]{0:T(128)S(1)} %copy-done.3, s32[16]{0:T(128)S(1)} %copy-done.4, s32[1]{0:T(128)S(6)} %copy.10.live, bf16[512,2048]{1,0:T(8,128)(2,1)S(1)} %copy-done, bf16[16,256,256]{2,1,0:T(8,128)(2,1)S(1)} %copy-done.1, f32[1,2048]{1,0:T(1,128)S(1)} %bitcast.2), custom_call_target="tpu_custom_call" | custom-call | tf_op jit(solution)/shard_map/step/pallas_call | solution.py:442
  83.3 1.3 %copy.11 = bf16[16,256,256]{2,1,0:T(8,128)(2,1)} copy(bf16[16,256,256]{2,1,0:T(8,128)(2,1)S(1)} %get-tuple-element.8) | data formatting | bytes 4194304
  84.6 0.6 copy.12
Async XLA Ops:
  1.3 1.6 %copy-start = (bf16[512,2048]{1,0:T(8,128)(2,1)S(1)}, bf16[512,2048]{1,0:T(8,128)(2,1)}, u32[]{:S(2)}) copy-start(bf16[512,2048]{1,0:T(8,128)(2,1)} %x.1) | copy-start | bytes 6291460
  2.9 1.6 %copy-start.1 = (bf16[16,256,256]{2,1,0:T(8,128)(2,1)S(1)}, bf16[16,256,256]{2,1,0:T(8,128)(2,1)}, u32[]{:S(2)}) copy-start(bf16[16,256,256]{2,1,0:T(8,128)(2,1)} %tiles_in.1) | copy-start | bytes 6291460
  4.5 0.7 copy-start.2
  5.2 0.7 copy-start.3
  5.8 0.7 copy-start.4

commit v4 on v3

--- a/solution.py
+++ b/solution.py
@@ -10,7 +10,7 @@
 B = 256
 STEP = 0.25
 PENALTY = 0.5
-VMEM_BYTES = 40 * 1024 * 1024
+VMEM_BYTES = 50 * 1024 * 1024
 
 
 class Place:
@@ -79,6 +79,7 @@
 
 
 HALVES = 2
+UNROLL = 4
 COPIES = 42
 
 
@@ -194,7 +195,7 @@
             copy.wait_recv()
 
     def sum_slots(self, acc, row, prev, last, tiles):
-        @pl.loop(0, tiles.shape[0])
+        @pl.loop(0, tiles.shape[0], unroll=UNROLL)
         def _(s):
             product = jnp.dot(self.ext[row[s]], tiles[s], preferred_element_type=jnp.float32)
             acc[s + 1] = acc[prev[s]] + product
@@ -285,10 +286,10 @@
 
 
 def step_kernel(
-    groups, row_in, col, live, x, tiles_in, diag_in, out, diag_out,
+    groups, row_hbm, col_hbm, live_hbm, x, tiles_in, diag_in, out, diag_out,
     ext_a, ext_b, img_a, img_b, own_a, own_b, part_a, part_b, core_a, core_b, chip_a, chip_b, half_a, half_b,
-    tiles, acc, x_turned, moved, diag_flat, diag, dots, dots_in, row, prev, last,
-    x_sem, tile_sem, diag_sem, send, recv,
+    tiles, acc, x_turned, moved, diag_flat, diag, dots, dots_in, row_in, col, live, row, prev, last,
+    index_sem, x_sem, tile_sem, diag_sem, send, recv,
 ):
     here = Place(groups)
     slots = tiles.shape[0]
@@ -312,6 +313,12 @@
     ]
     for load in loads[0] + loads[1]:
         load.start()
+    index_loads = [
+        pltpu.make_async_copy(src, dst, index_sem.at[i])
+        for i, (src, dst) in enumerate([(row_hbm, row_in), (col_hbm, col), (live_hbm, live)])
+    ]
+    for load in index_loads:
+        load.start()
     diag_load = pltpu.make_async_copy(diag_in, diag_flat, diag_sem)
     diag_load.start()
     tile_load = pltpu.make_async_copy(tiles_in, tiles, tile_sem)
@@ -320,6 +327,8 @@
     for load in loads[0]:
         load.wait()
     a.send_x()
+    for load in index_loads:
+        load.wait()
 
     def latest(column, end):
         def later(t, best):
@@ -346,7 +355,7 @@
     tile_load.wait()
 
     def turn(half, at):
-        @pl.loop(0, slots)
+        @pl.loop(0, slots, unroll=UNROLL)
         def _(s):
             x_turned[at, s] = half.ext[row[s]].T
 
@@ -391,7 +400,7 @@
     a.end_w()
 
     def first_half(start, end):
-        @pl.loop(start, end)
+        @pl.loop(start, end, unroll=UNROLL)
         def _(s):
             moved[s] = tiles[s].astype(jnp.float32) - scale * (own_grad(a, 0, s) + row_grad(a, s))
 
@@ -401,7 +410,7 @@
     b.pass_w(3)
     b.end_own_w()
 
-    @pl.loop(0, slots)
+    @pl.loop(0, slots, unroll=UNROLL)
     def _(s):
         moved[s] -= scale * own_grad(b, 1, s)
 
@@ -412,7 +421,7 @@
         diag_out[:, k * B : (k + 1) * B] = old - STEP * (total / samples - 1.0 / old)
     b.end_w()
 
-    @pl.loop(0, slots)
+    @pl.loop(0, slots, unroll=UNROLL)
     def _(s):
         value = moved[s] - scale * row_grad(b, s)
         kept = jnp.maximum(jnp.abs(value) - STEP * PENALTY, 0.0)
@@ -432,7 +441,6 @@
     owned = blocks // 4
     cut = samples // HALVES
     bf16, f32 = jnp.bfloat16, jnp.float32
-    smem = pl.BlockSpec(memory_space=pltpu.SMEM)
     vmem = pl.BlockSpec(memory_space=pltpu.VMEM)
     hbm = pl.BlockSpec(memory_space=pl.ANY)
 
@@ -445,7 +453,7 @@
             jax.ShapeDtypeStruct(tiles.shape, bf16),
             jax.ShapeDtypeStruct(diag.shape, f32),
         ),
-        in_specs=[smem, smem, smem, hbm, hbm, hbm],
+        in_specs=[hbm] * 6,
         out_specs=(vmem, vmem),
         scratch_shapes=twice(3 * blocks, cut, B)
         + twice(3 * blocks, B, cut)
@@ -465,7 +473,11 @@
             pltpu.VMEM((2, blocks, B), f32),
             pltpu.SMEM((slots,), jnp.int32),
             pltpu.SMEM((slots,), jnp.int32),
+            pltpu.SMEM((1,), jnp.int32),
+            pltpu.SMEM((slots,), jnp.int32),
+            pltpu.SMEM((slots,), jnp.int32),
             pltpu.SMEM((blocks,), jnp.int32),
+            pltpu.SemaphoreType.DMA((3,)),
             pltpu.SemaphoreType.DMA((2, blocks)),
             pltpu.SemaphoreType.DMA,
             pltpu.SemaphoreType.DMA,

time: 85.4 us -> 76.5 us (0.90)
  Pallas kernels: 76.8 us -> 71 us
  local copies, waits for them, and re-layouts: 7.1 us -> 3.92 us
    pallas_call x1, Pallas kernels: 76.8 us -> 71 us  [step(): pl.pallas_call(functools.partial(step_kernel, groups), out_shape=(jax.Sha...]
    unnamed x12 -> x8, local copies, waits for them, and re-layouts: 7.1 us -> 3.92 us
where the time goes in v4:
time: 76.5 us; the launch traced here: 76.2 us
  Pallas kernels  71 us (93%)
  local copies, waits for them, and re-layouts  3.92 us (5%)
  between operations  1.3 us (2%)
    pallas_call x1, Pallas kernels, step(): pl.pallas_call(functools.partial(step_kernel, groups), out_shape=(jax.Sha...  71 us
    unnamed x8, local copies, waits for them, and re-layouts  3.92 us

profile of v4, /device:TPU:3, one launch (start us, length us, event | category | flops | bytes accessed | tf_op | source)
XLA Modules:
  0.0 76.2 jit_solution(9837526131831465533)
XLA Ops:
  1.3 0.0 copy-start
  1.3 0.7 copy-done
  2.0 0.0 copy-start.1
  2.0 0.7 copy-done.1
  2.6 0.0 copy-start.2
  2.6 0.7 copy-done.2
  3.3 71.0 %step.1 = (bf16[16,256,256]{2,1,0:T(8,128)(2,1)S(1)}, f32[1,2048]{1,0:T(1,128)S(1)}) custom-call(s32[16]{0:T(128)S(1)} %copy-done.1, s32[16]{0:T(128)S(1)} %copy-done.2, s32[1]{0:T(128)S(6)} %copy.10.live_hbm, bf16[512,2048]{1,0:T(8,128)(2,1)} %x.1, bf16[16,256,256]{2,1,0:T(8,128)(2,1)} %tiles_in.1, f32[1,2048]{1,0:T(1,128)S(1)} %bitcast.2), custom_call_target="tpu_custom_call" | custom-call | tf_op jit(solution)/shard_map/step/pallas_call | solution.py:450
  74.3 1.3 %copy.11 = bf16[16,256,256]{2,1,0:T(8,128)(2,1)} copy(bf16[16,256,256]{2,1,0:T(8,128)(2,1)S(1)} %get-tuple-element.8) | data formatting | bytes 4194304
  75.6 0.6 copy.12
Async XLA Ops:
  1.3 0.7 copy-start
  2.0 0.7 copy-start.1
  2.6 0.7 copy-start.2

commit v5 on v4

--- a/solution.py
+++ b/solution.py
@@ -78,12 +78,12 @@
     )
 
 
-HALVES = 2
+PARTS = 4
 UNROLL = 4
 COPIES = 42
 
 
-class Half:
+class Part:
     def __init__(self, here, first, ext, img, own_img, part, core_in, chip_sum, half_in, send, recv):
         self.here = here
         self.ext, self.img, self.own_img = ext, img, own_img
@@ -285,34 +285,36 @@
                 copy.wait_send()
 
 
-def step_kernel(
-    groups, row_hbm, col_hbm, live_hbm, x, tiles_in, diag_in, out, diag_out,
-    ext_a, ext_b, img_a, img_b, own_a, own_b, part_a, part_b, core_a, core_b, chip_a, chip_b, half_a, half_b,
-    tiles, acc, x_turned, moved, diag_flat, diag, dots, dots_in, row_in, col, live, row, prev, last,
-    index_sem, x_sem, tile_sem, diag_sem, send, recv,
-):
+def step_kernel(groups, row_hbm, col_hbm, live_hbm, x, tiles_in, diag_in, out, diag_out, *scratch):
+    own_refs, shared_refs = scratch[: 7 * PARTS], scratch[7 * PARTS :]
+    (
+        tiles, acc, x_turned, moved, diag_flat, diag, dots, dots_in, row_in, col, live, row, prev, last,
+        index_sem, x_sem, tile_sem, diag_sem, send, recv,
+    ) = shared_refs
     here = Place(groups)
     slots = tiles.shape[0]
     samples = x.shape[0]
     blocks = x.shape[1] // B
-    cut = samples // HALVES
+    cut = samples // PARTS
     scale = STEP / (2.0 * samples)
-    a = Half(here, 0, ext_a, img_a, own_a, part_a, core_a, chip_a, half_a, send, recv)
-    b = Half(here, COPIES, ext_b, img_b, own_b, part_b, core_b, chip_b, half_b, send, recv)
-    dots_core = remote(dots.at[0], dots_in.at[0], send, recv, 2 * COPIES, here.to_core())
-    dots_half = remote(dots.at[1], dots_in.at[1], send, recv, 2 * COPIES + 1, here.to_half())
+    parts = [
+        Part(here, p * COPIES, *[own_refs[i * PARTS + p] for i in range(7)], send, recv) for p in range(PARTS)
+    ]
+    dots_core = remote(dots.at[0], dots_in.at[0], send, recv, PARTS * COPIES, here.to_core())
+    dots_half = remote(dots.at[1], dots_in.at[1], send, recv, PARTS * COPIES + 1, here.to_half())
 
     loads = [
         [
             pltpu.make_async_copy(
-                x.at[h * cut : (h + 1) * cut, k * B : (k + 1) * B], half.ext.at[blocks + k], x_sem.at[h, k]
+                x.at[p * cut : (p + 1) * cut, k * B : (k + 1) * B], part.ext.at[blocks + k], x_sem.at[p, k]
             )
             for k in range(blocks)
         ]
-        for h, half in enumerate([a, b])
+        for p, part in enumerate(parts)
     ]
-    for load in loads[0] + loads[1]:
-        load.start()
+    for part_loads in loads:
+        for load in part_loads:
+            load.start()
     index_loads = [
         pltpu.make_async_copy(src, dst, index_sem.at[i])
         for i, (src, dst) in enumerate([(row_hbm, row_in), (col_hbm, col), (live_hbm, live)])
@@ -326,7 +328,7 @@
     here.greet()
     for load in loads[0]:
         load.wait()
-    a.send_x()
+    parts[0].send_x()
     for load in index_loads:
         load.wait()
 
@@ -350,86 +352,109 @@
     diag_load.wait()
     for k in range(blocks):
         diag[k : k + 1, :] = diag_flat[:, k * B : (k + 1) * B]
-    for load in loads[1]:
-        load.wait()
+    for part_loads in loads[1:]:
+        for load in part_loads:
+            load.wait()
     tile_load.wait()
 
-    def turn(half, at):
+    def turn(pair):
         @pl.loop(0, slots, unroll=UNROLL)
         def _(s):
-            x_turned[at, s] = half.ext[row[s]].T
-
-    def own_grad(half, at, s):
+            both = [parts[2 * pair + i].ext[row[s]] for i in range(2)]
+            x_turned[pair, s] = jnp.concatenate(both, axis=0).T
+
+    def own_grad(pair, s):
+        image = [parts[2 * pair + i].own_img[col[s]] for i in range(2)]
         return lax.dot_general(
-            x_turned[at, s], half.own_img[col[s]], (((1,), (1,)), ((), ())),
+            x_turned[pair, s], jnp.concatenate(image, axis=1), (((1,), (1,)), ((), ())),
             preferred_element_type=jnp.float32,
         )
 
-    def row_grad(half, s):
-        return jnp.dot(half.img[row[s]], half.ext[blocks + col[s]], preferred_element_type=jnp.float32)
-
-    for k in range(3):
-        a.pass_x(k)
-    b.send_x()
-    a.end_x()
-    b.pass_x(0)
-    a.sum_slots(acc, row, prev, last, tiles)
-    b.pass_x(1)
-    a.sum_chip()
-    b.pass_x(2)
-    turn(a, 0)
-    b.end_x()
-    b.sum_slots(acc, row, prev, last, tiles)
-    a.finish_image(diag, dots)
-    b.sum_chip()
-    for e in range(2):
-        a.pass_gathered(e)
-        a.pass_w(e)
-    turn(b, 1)
-    b.finish_image(diag, dots)
+    def row_grad(pair, s):
+        image = [parts[2 * pair + i].img[row[s]] for i in range(2)]
+        data = [parts[2 * pair + i].ext[blocks + col[s]] for i in range(2)]
+        return jnp.dot(
+            jnp.concatenate(image, axis=1), jnp.concatenate(data, axis=0),
+            preferred_element_type=jnp.float32,
+        )
+
+    def pass_first(part):
+        for e in range(2):
+            part.pass_gathered(e)
+            part.pass_w(e)
+
+    def pass_second(part):
+        part.pass_w(2)
+        part.pass_w(3)
+
+    for t in range(PARTS):
+        parts[t].pass_x(0)
+        if t + 1 < PARTS:
+            parts[t + 1].send_x()
+        parts[t].pass_x(1)
+        parts[t].pass_x(2)
+        if t >= 1:
+            parts[t - 1].sum_chip()
+        if t >= 2:
+            parts[t - 2].finish_image(diag, dots)
+        if t >= 3:
+            pass_first(parts[t - 3])
+        parts[t].end_x()
+        parts[t].sum_slots(acc, row, prev, last, tiles)
+    p0, p1, p2, p3 = parts
+    p3.sum_chip()
+    p2.finish_image(diag, dots)
+    pass_first(p1)
+    pass_second(p0)
+    turn(0)
+    p3.finish_image(diag, dots)
     dots_core.start()
-    a.pass_w(2)
-    a.pass_w(3)
-    for e in range(2):
-        b.pass_gathered(e)
-        b.pass_w(e)
+    pass_first(p2)
+    pass_second(p1)
+    p0.end_own_w()
+    p0.end_w()
+    pass_first(p3)
+    pass_second(p2)
     dots_core.wait_recv()
     dots[1] = dots[0] + dots_in[0]
     dots_half.start()
-    a.end_own_w()
-    a.end_w()
-
-    def first_half(start, end):
+    turn(1)
+    p1.end_own_w()
+    p1.end_w()
+
+    def first_pair(start, end):
         @pl.loop(start, end, unroll=UNROLL)
         def _(s):
-            moved[s] = tiles[s].astype(jnp.float32) - scale * (own_grad(a, 0, s) + row_grad(a, s))
-
-    first_half(0, slots // 2)
-    b.pass_w(2)
-    first_half(slots // 2, slots)
-    b.pass_w(3)
-    b.end_own_w()
+            moved[s] = tiles[s].astype(jnp.float32) - scale * (own_grad(0, s) + row_grad(0, s))
+
+    first_pair(0, slots // 2)
+    p3.pass_w(2)
+    first_pair(slots // 2, slots)
+    p3.pass_w(3)
+    p2.end_own_w()
+    p3.end_own_w()
 
     @pl.loop(0, slots, unroll=UNROLL)
     def _(s):
-        moved[s] -= scale * own_grad(b, 1, s)
+        moved[s] -= scale * own_grad(1, s)
 
     dots_half.wait_recv()
     for k in range(blocks):
         total = dots[1, k : k + 1, :] + dots_in[1, k : k + 1, :]
         old = diag[k : k + 1, :]
         diag_out[:, k * B : (k + 1) * B] = old - STEP * (total / samples - 1.0 / old)
-    b.end_w()
+    p2.end_w()
+    p3.end_w()
 
     @pl.loop(0, slots, unroll=UNROLL)
     def _(s):
-        value = moved[s] - scale * row_grad(b, s)
+        value = moved[s] - scale * row_grad(1, s)
         kept = jnp.maximum(jnp.abs(value) - STEP * PENALTY, 0.0)
         signed = jnp.where(value < 0, -kept, kept)
         out[s] = jnp.where(s < live[0], signed, 0.0).astype(out.dtype)
 
-    a.drain()
-    b.drain()
+    for part in parts:
+        part.drain()
     dots_core.wait_send()
     dots_half.wait_send()
 
@@ -439,13 +464,13 @@
     slots = tiles.shape[0]
     blocks = width // B
     owned = blocks // 4
-    cut = samples // HALVES
+    cut = samples // PARTS
     bf16, f32 = jnp.bfloat16, jnp.float32
     vmem = pl.BlockSpec(memory_space=pltpu.VMEM)
     hbm = pl.BlockSpec(memory_space=pl.ANY)
 
-    def twice(*shape):
-        return [pltpu.VMEM(shape, bf16)] * 2
+    def each(*shape):
+        return [pltpu.VMEM(shape, bf16)] * PARTS
 
     return pl.pallas_call(
         functools.partial(step_kernel, groups),
@@ -455,17 +480,17 @@
         ),
         in_specs=[hbm] * 6,
         out_specs=(vmem, vmem),
-        scratch_shapes=twice(3 * blocks, cut, B)
-        + twice(3 * blocks, B, cut)
-        + twice(blocks, B, cut)
-        + twice(blocks, cut, B)
-        + twice(2, owned, cut, B)
-        + twice(owned, cut, B)
-        + twice(owned, cut, B)
+        scratch_shapes=each(3 * blocks, cut, B)
+        + each(3 * blocks, B, cut)
+        + each(blocks, B, cut)
+        + each(blocks, cut, B)
+        + each(2, owned, cut, B)
+        + each(owned, cut, B)
+        + each(owned, cut, B)
         + [
             pltpu.VMEM(tiles.shape, bf16),
             pltpu.VMEM((slots + 1, cut, B), f32),
-            pltpu.VMEM((2, slots, B, cut), bf16),
+            pltpu.VMEM((PARTS // 2, slots, B, 2 * cut), bf16),
             pltpu.VMEM((slots, B, B), f32),
             pltpu.VMEM(diag.shape, f32),
             pltpu.VMEM((blocks, B), f32),
@@ -478,11 +503,11 @@
             pltpu.SMEM((slots,), jnp.int32),
             pltpu.SMEM((blocks,), jnp.int32),
             pltpu.SemaphoreType.DMA((3,)),
-            pltpu.SemaphoreType.DMA((2, blocks)),
+            pltpu.SemaphoreType.DMA((PARTS, blocks)),
             pltpu.SemaphoreType.DMA,
             pltpu.SemaphoreType.DMA,
-            pltpu.SemaphoreType.DMA((2 * COPIES + 2,)),
-            pltpu.SemaphoreType.DMA((2 * COPIES + 2,)),
+            pltpu.SemaphoreType.DMA((PARTS * COPIES + 2,)),
+            pltpu.SemaphoreType.DMA((PARTS * COPIES + 2,)),
         ],
         compiler_params=pltpu.CompilerParams(
             collective_id=0, has_side_effects=True, vmem_limit_bytes=VMEM_BYTES

time: 76.5 us -> 86 us (1.12)
  Pallas kernels: 71 us -> 80.5 us
    pallas_call x1, Pallas kernels: 71 us -> 80.5 us  [step(): pl.pallas_call(functools.partial(step_kernel, groups), out_shape=(jax.Sha...]
where the time goes in v5:
time: 86 us; the launch traced here: 85.8 us
  Pallas kernels  80.5 us (94%)
  local copies, waits for them, and re-layouts  3.92 us (5%)
  between operations  1.3 us (2%)
    pallas_call x1, Pallas kernels, step(): pl.pallas_call(functools.partial(step_kernel, groups), out_shape=(jax.Sha...  80.5 us
    unnamed x8, local copies, waits for them, and re-layouts  3.92 us

profile of v5, /device:TPU:3, one launch (start us, length us, event | category | flops | bytes accessed | tf_op | source)
XLA Modules:
  0.0 85.8 jit_solution(1229904783788162989)
XLA Ops:
  1.3 0.0 copy-start
  1.3 0.7 copy-done
  2.0 0.0 copy-start.1
  2.0 0.7 copy-done.1
  2.6 0.0 copy-start.2
  2.6 0.7 copy-done.2
  3.3 80.5 %step.1 = (bf16[16,256,256]{2,1,0:T(8,128)(2,1)S(1)}, f32[1,2048]{1,0:T(1,128)S(1)}) custom-call(s32[16]{0:T(128)S(1)} %copy-done.1, s32[16]{0:T(128)S(1)} %copy-done.2, s32[1]{0:T(128)S(6)} %copy.10.live_hbm, bf16[512,2048]{1,0:T(8,128)(2,1)} %x.1, bf16[16,256,256]{2,1,0:T(8,128)(2,1)} %tiles_in.1, f32[1,2048]{1,0:T(1,128)S(1)} %bitcast.2), custom_call_target="tpu_custom_call" | custom-call | tf_op jit(solution)/shard_map/step/pallas_call | solution.py:475
  83.8 1.3 %copy.11 = bf16[16,256,256]{2,1,0:T(8,128)(2,1)} copy(bf16[16,256,256]{2,1,0:T(8,128)(2,1)S(1)} %get-tuple-element.8) | data formatting | bytes 4194304
  85.2 0.6 copy.12
Async XLA Ops:
  1.3 0.7 copy-start
  2.0 0.7 copy-start.1
  2.6 0.7 copy-start.2

commit v6 on v4

--- a/solution.py
+++ b/solution.py
@@ -91,12 +91,9 @@
         blocks, samples, _ = part.shape
         unit = samples // 8
         near, far = here.near, here.far
-        self.mine = 2 * here.half + here.core
-        self.other = 2 * (1 - here.half) + here.core
-        self.mine_core = 2 * here.half + 1 - here.core
-        self.other_core = 2 * (1 - here.half) + 1 - here.core
-        self.owned = blocks // 4
-        owned = self.owned
+        self.owned = blocks // 2
+        self.first = here.core * self.owned
+        self.first_core = (1 - here.core) * self.owned
 
         def copy(src, dst, at, device):
             return remote(src, dst, send, recv, first + at, device)
@@ -123,38 +120,37 @@
             for s, at in [(near, 8), (far, 12)]
         ]
 
-        def img_at(section, q, e):
-            return img.at[section * blocks + q * owned + e]
-
-        def own_at(q, e):
-            return own_img.at[q * owned + e]
-
+        def img_at(section, e):
+            return img.at[section * blocks + self.first + e]
+
+        def own_at(e):
+            return own_img.at[self.first + e]
+
+        self.pieces = self.owned // 2
         self.to_core = [
-            copy(part.at[pl.ds(q * owned, owned)], core_in.at[j], 16 + j, here.to_core())
-            for j, q in enumerate([self.other_core, self.mine_core])
-        ]
-        self.to_half = [copy(chip_sum.at[e], half_in.at[e], 18 + e, here.to_half()) for e in range(2)]
-        self.gather = [
-            copy(own_at(self.mine, e), own_at(self.mine, e), 20 + e, here.to_half()) for e in range(2)
-        ]
-        places = [(self.mine, 0), (self.mine, 1), (self.other, 0), (self.other, 1)]
+            copy(
+                part.at[pl.ds(self.first_core + i * self.pieces, self.pieces)],
+                core_in.at[pl.ds(i * self.pieces, self.pieces)],
+                16 + i,
+                here.to_core(),
+            )
+            for i in range(2)
+        ]
+        every = range(self.owned)
+        size = self.owned
+        self.to_half = [copy(chip_sum.at[e], half_in.at[e], 18 + e, here.to_half()) for e in every]
         self.partner_w = [
-            copy(own_at(q, e), img_at(far, q, e), 22 + i, here.to_partner())
-            for i, (q, e) in enumerate(places)
+            copy(own_at(e), img_at(far, e), 18 + size + e, here.to_partner()) for e in every
         ]
         self.relay_w = [
-            copy(img_at(near, q, e), img_at(far, q, e), 26 + i, here.to_target())
-            for i, (q, e) in enumerate(places)
+            copy(img_at(near, e), img_at(far, e), 18 + 2 * size + e, here.to_target()) for e in every
         ]
         self.share_own_w = [
-            copy(own_at(q, e), own_at(q, e), 30 + i, here.to_core()) for i, (q, e) in enumerate(places)
+            copy(own_at(e), own_at(e), 18 + 3 * size + e, here.to_core()) for e in every
         ]
         self.share_near_w, self.share_far_w = [
-            [
-                copy(img_at(s, q, e), img_at(s, q, e), at + i, here.to_core())
-                for i, (q, e) in enumerate(places)
-            ]
-            for s, at in [(near, 34), (far, 38)]
+            [copy(img_at(s, e), img_at(s, e), 18 + at * size + e, here.to_core()) for e in every]
+            for s, at in [(near, 4), (far, 5)]
         ]
 
     def send_x(self):
@@ -200,41 +196,34 @@
             product = jnp.dot(self.ext[row[s]], tiles[s], preferred_element_type=jnp.float32)
             acc[s + 1] = acc[prev[s]] + product
 
-        for j, q in enumerate([self.other_core, self.mine_core, self.other, self.mine]):
-            for e in range(2):
-                k = q * self.owned + e
+        for i in range(2):
+            for e in range(self.pieces):
+                k = self.first_core + i * self.pieces + e
                 self.part[k] = acc[last[k]].astype(jnp.bfloat16)
-            if j < 2:
-                self.to_core[j].start()
+            self.to_core[i].start()
+        for e in range(self.owned):
+            k = self.first + e
+            self.part[k] = acc[last[k]].astype(jnp.bfloat16)
 
     def sum_chip(self):
-        self.to_core[0].wait_recv()
-        for e in range(2):
-            both = self.part[self.other * self.owned + e].astype(jnp.float32)
-            both = both + self.core_in[0, e].astype(jnp.float32)
+        for e in range(self.owned):
+            if e % self.pieces == 0:
+                self.to_core[e // self.pieces].wait_recv()
+            both = self.part[self.first + e].astype(jnp.float32) + self.core_in[e].astype(jnp.float32)
             self.chip_sum[e] = both.astype(jnp.bfloat16)
             self.to_half[e].start()
 
-    def finish_image(self, diag, dots):
-        self.to_core[1].wait_recv()
+    def finish_image(self, e, diag, dots):
         blocks = self.part.shape[0]
-        for e in range(2):
-            self.to_half[e].wait_recv()
-            k = self.mine * self.owned + e
-            xs = self.ext[blocks + k].astype(jnp.float32)
-            both = self.part[k].astype(jnp.float32) + self.core_in[1, e].astype(jnp.float32)
-            both = both + self.half_in[e].astype(jnp.float32) + xs * diag[pl.ds(k, 1), :]
-            rounded = both.astype(jnp.bfloat16)
-            self.own_img[k] = rounded.T
-            self.partner_w[e].start()
-            self.gather[e].start()
-            self.share_own_w[e].start()
-            dots[0, pl.ds(k, 1), :] += jnp.sum(xs * rounded.astype(jnp.float32), axis=0, keepdims=True)
-
-    def pass_gathered(self, e):
-        self.gather[e].wait_recv()
-        self.partner_w[2 + e].start()
-        self.share_own_w[2 + e].start()
+        self.to_half[e].wait_recv()
+        k = self.first + e
+        xs = self.ext[blocks + k].astype(jnp.float32)
+        both = self.chip_sum[e].astype(jnp.float32) + self.half_in[e].astype(jnp.float32)
+        rounded = (both + xs * diag[pl.ds(k, 1), :]).astype(jnp.bfloat16)
+        self.own_img[k] = rounded.T
+        self.partner_w[e].start()
+        self.share_own_w[e].start()
+        dots[0, pl.ds(k, 1), :] += jnp.sum(xs * rounded.astype(jnp.float32), axis=0, keepdims=True)
 
     def pass_w(self, i):
         self.partner_w[i].wait_recv()
@@ -257,7 +246,7 @@
     def end_w(self):
         @pl.when(self.here.has_source)
         def _():
-            for i in range(4):
+            for i in range(self.owned):
                 self.relay_w[i].wait_recv()
                 self.share_far_w[i].start()
             for copy in self.share_far_w:
@@ -268,7 +257,7 @@
 
     def drain(self):
         for copies in [
-            self.partner, self.share_near, self.across[:1], self.to_core, self.to_half, self.gather,
+            self.partner, self.share_near, self.across[:1], self.to_core, self.to_half,
             self.partner_w, self.share_own_w, self.share_near_w,
         ]:
             for copy in copies:
@@ -299,8 +288,7 @@
     scale = STEP / (2.0 * samples)
     a = Half(here, 0, ext_a, img_a, own_a, part_a, core_a, chip_a, half_a, send, recv)
     b = Half(here, COPIES, ext_b, img_b, own_b, part_b, core_b, chip_b, half_b, send, recv)
-    dots_core = remote(dots.at[0], dots_in.at[0], send, recv, 2 * COPIES, here.to_core())
-    dots_half = remote(dots.at[1], dots_in.at[1], send, recv, 2 * COPIES + 1, here.to_half())
+    dots_core = remote(dots.at[0], dots_in, send, recv, 2 * COPIES, here.to_core())
 
     loads = [
         [
@@ -380,23 +368,20 @@
     turn(a, 0)
     b.end_x()
     b.sum_slots(acc, row, prev, last, tiles)
-    a.finish_image(diag, dots)
+    a.finish_image(0, diag, dots)
+    a.finish_image(1, diag, dots)
     b.sum_chip()
-    for e in range(2):
-        a.pass_gathered(e)
-        a.pass_w(e)
+    a.pass_w(0)
+    a.finish_image(2, diag, dots)
+    a.pass_w(1)
+    a.finish_image(3, diag, dots)
+    a.pass_w(2)
     turn(b, 1)
-    b.finish_image(diag, dots)
-    dots_core.start()
-    a.pass_w(2)
+    b.finish_image(0, diag, dots)
     a.pass_w(3)
-    for e in range(2):
-        b.pass_gathered(e)
-        b.pass_w(e)
-    dots_core.wait_recv()
-    dots[1] = dots[0] + dots_in[0]
-    dots_half.start()
     a.end_own_w()
+    b.finish_image(1, diag, dots)
+    b.pass_w(0)
     a.end_w()
 
     def first_half(start, end):
@@ -404,9 +389,15 @@
         def _(s):
             moved[s] = tiles[s].astype(jnp.float32) - scale * (own_grad(a, 0, s) + row_grad(a, s))
 
-    first_half(0, slots // 2)
+    step_size = slots // 4
+    first_half(0, step_size)
+    b.finish_image(2, diag, dots)
+    b.pass_w(1)
+    first_half(step_size, 2 * step_size)
+    b.finish_image(3, diag, dots)
+    dots_core.start()
     b.pass_w(2)
-    first_half(slots // 2, slots)
+    first_half(2 * step_size, slots)
     b.pass_w(3)
     b.end_own_w()
 
@@ -414,9 +405,9 @@
     def _(s):
         moved[s] -= scale * own_grad(b, 1, s)
 
-    dots_half.wait_recv()
+    dots_core.wait_recv()
     for k in range(blocks):
-        total = dots[1, k : k + 1, :] + dots_in[1, k : k + 1, :]
+        total = dots[0, k : k + 1, :] + dots_in[k : k + 1, :]
         old = diag[k : k + 1, :]
         diag_out[:, k * B : (k + 1) * B] = old - STEP * (total / samples - 1.0 / old)
     b.end_w()
@@ -431,14 +422,13 @@
     a.drain()
     b.drain()
     dots_core.wait_send()
-    dots_half.wait_send()
 
 
 def step(x, tiles, diag, row, col, live, groups):
     samples, width = x.shape
     slots = tiles.shape[0]
     blocks = width // B
-    owned = blocks // 4
+    owned = blocks // 2
     cut = samples // HALVES
     bf16, f32 = jnp.bfloat16, jnp.float32
     vmem = pl.BlockSpec(memory_space=pltpu.VMEM)
@@ -459,7 +449,7 @@
         + twice(3 * blocks, B, cut)
         + twice(blocks, B, cut)
         + twice(blocks, cut, B)
-        + twice(2, owned, cut, B)
+        + twice(owned, cut, B)
         + twice(owned, cut, B)
         + twice(owned, cut, B)
         + [
@@ -469,8 +459,8 @@
             pltpu.VMEM((slots, B, B), f32),
             pltpu.VMEM(diag.shape, f32),
             pltpu.VMEM((blocks, B), f32),
-            pltpu.VMEM((2, blocks, B), f32),
-            pltpu.VMEM((2, blocks, B), f32),
+            pltpu.VMEM((1, blocks, B), f32),
+            pltpu.VMEM((blocks, B), f32),
             pltpu.SMEM((slots,), jnp.int32),
             pltpu.SMEM((slots,), jnp.int32),
             pltpu.SMEM((1,), jnp.int32),

time: 76.5 us -> 82.4 us (1.077); the launches traced: 76.2 us -> 81.2 us
  Pallas kernels: 71 us -> 75.9 us
    pallas_call x1, Pallas kernels: 71 us -> 75.9 us  [step(): pl.pallas_call(functools.partial(step_kernel, groups), out_shape=(jax.Sha...]
where the time goes in v6:
time: 82.4 us; the launch traced here: 81.2 us
  Pallas kernels  75.9 us (92%)
  local copies, waits for them, and re-layouts  3.92 us (5%)
  between operations  1.3 us (2%)
    pallas_call x1, Pallas kernels, step(): pl.pallas_call(functools.partial(step_kernel, groups), out_shape=(jax.Sha...  75.9 us
    unnamed x8, local copies, waits for them, and re-layouts  3.92 us

profile of v6, /device:TPU:3, one launch (start us, length us, event | category | flops | bytes accessed | tf_op | source)
XLA Modules:
  0.0 81.2 jit_solution(14483787884155594835)
XLA Ops:
  1.3 0.0 copy-start
  1.3 0.7 copy-done
  2.0 0.0 copy-start.1
  2.0 0.7 copy-done.1
  2.6 0.0 copy-start.2
  2.6 0.7 copy-done.2
  3.3 75.9 %step.1 = (bf16[16,256,256]{2,1,0:T(8,128)(2,1)S(1)}, f32[1,2048]{1,0:T(1,128)S(1)}) custom-call(s32[16]{0:T(128)S(1)} %copy-done.1, s32[16]{0:T(128)S(1)} %copy-done.2, s32[1]{0:T(128)S(6)} %copy.10.live_hbm, bf16[512,2048]{1,0:T(8,128)(2,1)} %x.1, bf16[16,256,256]{2,1,0:T(8,128)(2,1)} %tiles_in.1, f32[1,2048]{1,0:T(1,128)S(1)} %bitcast.2), custom_call_target="tpu_custom_call" | custom-call | tf_op jit(solution)/shard_map/step/pallas_call | solution.py:440
  79.2 1.3 %copy.11 = bf16[16,256,256]{2,1,0:T(8,128)(2,1)} copy(bf16[16,256,256]{2,1,0:T(8,128)(2,1)S(1)} %get-tuple-element.8) | data formatting | bytes 4194304
  80.6 0.6 copy.12
Async XLA Ops:
  1.3 0.7 copy-start
  2.0 0.7 copy-start.1
  2.6 0.7 copy-start.2

commit v7 on v4

--- a/solution.py
+++ b/solution.py
@@ -79,7 +79,7 @@
 
 
 HALVES = 2
-UNROLL = 4
+UNROLL = 8
 COPIES = 42
 
 

time: 76.5 us -> 75.9 us (level)
  no operation moved by 1% of the time
where the time goes in v7:
time: 75.9 us; the launch traced here: 75.7 us
  Pallas kernels  70.5 us (93%)
  local copies, waits for them, and re-layouts  3.92 us (5%)
  between operations  1.3 us (2%)
    pallas_call x1, Pallas kernels, step(): pl.pallas_call(functools.partial(step_kernel, groups), out_shape=(jax.Sha...  70.5 us
    unnamed x8, local copies, waits for them, and re-layouts  3.92 us

profile of v7, /device:TPU:3, one launch (start us, length us, event | category | flops | bytes accessed | tf_op | source)
XLA Modules:
  0.0 75.7 jit_solution(8925553524237853689)
XLA Ops:
  1.3 0.0 copy-start
  1.3 0.7 copy-done
  2.0 0.0 copy-start.1
  2.0 0.7 copy-done.1
  2.6 0.0 copy-start.2
  2.6 0.7 copy-done.2
  3.3 70.5 %step.1 = (bf16[16,256,256]{2,1,0:T(8,128)(2,1)S(1)}, f32[1,2048]{1,0:T(1,128)S(1)}) custom-call(s32[16]{0:T(128)S(1)} %copy-done.1, s32[16]{0:T(128)S(1)} %copy-done.2, s32[1]{0:T(128)S(6)} %copy.10.live_hbm, bf16[512,2048]{1,0:T(8,128)(2,1)} %x.1, bf16[16,256,256]{2,1,0:T(8,128)(2,1)} %tiles_in.1, f32[1,2048]{1,0:T(1,128)S(1)} %bitcast.2), custom_call_target="tpu_custom_call" | custom-call | tf_op jit(solution)/shard_map/step/pallas_call | solution.py:450
  73.8 1.3 %copy.11 = bf16[16,256,256]{2,1,0:T(8,128)(2,1)} copy(bf16[16,256,256]{2,1,0:T(8,128)(2,1)S(1)} %get-tuple-element.8) | data formatting | bytes 4194304
  75.1 0.6 copy.12
Async XLA Ops:
  1.3 0.7 copy-start
  2.0 0.7 copy-start.1
  2.6 0.7 copy-start.2
